TPU v7x, 128 devices: a whole 4x4x4 slice. The times are simulated.
128 devices in a mesh: lat: 64 (over x, y, z), lev: 2 (over core).
Axes of the slice: x: 4, y: 4, z: 4, core: 2. Of those that a mesh axis runs over, the one named last changes fastest.
Arguments:
- fourier: bfloat16 [640, 2, 4, 16, 1536], P('lat', None, None, 'lev'), may hold values from -6 to 6
- vertical_band: float32 [4, 16, 5], replicated, may hold values from -3 to 3
- cycle_points: int32 [640], P('lat'), may hold values from 20 to 3091
- legendre: bfloat16 [768, 2, 640, 640], P(('lat', 'lev')), may hold values from -0.25 to 0.25
- wave_of_slot: int32 [768], replicated, may hold values from 0 to 767, as said below
Outputs:
- spectral: bfloat16 [768, 2, 640, 128], P(('lat', 'lev'))
Inputs may be any that keep to these rules, and one draw needn't show every extreme that they name: A permutation of the wavenumbers: slot q of legendre and spectral belongs to wavenumber wave_of_slot[q]. The device runs of 6 slots take wavenumbers dealt in rounds of alternating direction. Wavenumber m is resolved on the cycles of pair j where 2 m < cycle_points[j].
All inputs are finite; a program needn't handle non-finite values.
Results may differ from a plain program's by a relative error of at most 0.001.
Values may be sent and summed in bfloat16 or wider, within the bound.
No kernel may reach another device: no remote copies, remote signals or barrier semaphores. Data moves between devices by JAX's collectives and lax.ppermute only.
A program may use at most 320 MiB of HBM per device.

v0:
```python
import jax
import jax.numpy as jnp
from jax import lax
from jax.sharding import PartitionSpec as P


def with_halo(block, sides, width):
    for axis, dim in sides:
        count = lax.axis_size(axis)
        forward = [(i, i + 1) for i in range(count - 1)]
        backward = [(target, source) for source, target in forward]
        low = lax.ppermute(
            lax.slice_in_dim(block, block.shape[dim] - width, None, axis=dim), axis, forward
        )
        high = lax.ppermute(lax.slice_in_dim(block, 0, width, axis=dim), axis, backward)
        block = jnp.concatenate([low, block, high], axis=dim)
    return block


def apply_band(padded, band_padded, level_start, count, reach, level_dim):
    fields = band_padded.shape[0]
    out_shape = list(padded.shape)
    out_shape[level_dim] = count
    total = jnp.zeros(tuple(out_shape), jnp.float32)
    shape = [1] * len(out_shape)
    shape[level_dim - 1] = fields
    shape[level_dim] = count
    for offset in range(2 * reach + 1):
        first = 2 * reach - offset
        weights = lax.dynamic_slice_in_dim(band_padded, level_start + first, count, 1)[:, :, offset]
        shifted = lax.slice_in_dim(padded, first, first + count, axis=level_dim).astype(jnp.float32)
        total = total + weights.reshape(tuple(shape)) * shifted
    return total


def to_columns(product, fields):
    shape = product.shape
    groups = shape[-2]
    inner = shape[-1] // fields
    split = product.reshape(shape[:-2] + (groups, fields, inner))
    count = len(split.shape)
    order = list(range(count - 3)) + [count - 2, count - 3, count - 1]
    return jnp.transpose(split, tuple(order)).reshape(shape[:-2] + (groups * fields * inner,))


def body(fourier, vertical_band, cycle_points, legendre, wave_of_slot):
    pairs_here, sides, fields, levels_here, columns = fourier.shape
    waves = columns // 2
    reach = (vertical_band.shape[2] - 1) // 2
    slots_here = legendre.shape[0]
    half_rows = legendre.shape[2]
    lat_count = lax.axis_size("lat")
    lev_count = lax.axis_size("lev")
    band_padded = jnp.pad(vertical_band, ((0, 0), (reach, reach), (0, 0)))
    padded = with_halo(fourier, (("lev", 3),), reach)
    level_start = lax.axis_index("lev") * levels_here
    source = apply_band(padded, band_padded, level_start, levels_here, reach, 3)
    column_wave = lax.broadcasted_iota(jnp.int32, (1, columns), 1) % waves
    keep = (2 * column_wave < cycle_points[:, None]).astype(jnp.float32)
    masked = source * keep[:, None, None, None, :]
    folded = jnp.stack([masked[:, 0] + masked[:, 1], masked[:, 0] - masked[:, 1]], axis=1)
    picked = jnp.concatenate([wave_of_slot, wave_of_slot + waves])
    ordered = jnp.take(folded, picked, axis=4)
    split = ordered.reshape(pairs_here, 2, fields, levels_here, 2, waves)
    outgoing = jnp.transpose(split, (5, 1, 0, 2, 3, 4)).reshape(
        waves, 2, pairs_here * fields * levels_here * 2
    )
    arrived = lax.all_to_all(outgoing, ("lat", "lev"), split_axis=0, concat_axis=2, tiled=True)
    right = arrived.reshape(
        slots_here, 2, lat_count, lev_count, pairs_here, fields * levels_here * 2
    )
    form = "skap,savpc->skvc"
    table_all = legendre.reshape(slots_here, 2, half_rows, lat_count, pairs_here)
    own_waves = lax.dynamic_slice_in_dim(
        wave_of_slot, lax.axis_index(("lat", "lev")) * slots_here, slots_here
    )
    degree_limit = 2 * half_rows
    product = jnp.einsum(
        "q" + form.replace(",", ",q").replace("->", "->q"),
        table_all.astype(jnp.float32),
        right,
        precision=lax.Precision.HIGHEST,
    )
    product = to_columns(product, fields)
    degree_rows = lax.broadcasted_iota(jnp.int32, (1, 1, half_rows), 2)
    parity = lax.broadcasted_iota(jnp.int32, (1, 2, 1), 1)
    valid = own_waves[:, None, None] + 2 * degree_rows + parity < degree_limit
    spectral = jnp.where(valid[..., None], product, 0.0).astype(jnp.bfloat16)
    return spectral


def solution(mesh):
    in_specs = (
        P("lat", None, None, "lev", None),
        P(),
        P("lat"),
        P(("lat", "lev"), None, None, None),
        P(),
    )
    out_specs = P(("lat", "lev"), None, None, None)
    return jax.shard_map(body, mesh=mesh, in_specs=in_specs, out_specs=out_specs, check_vma=False)
```

profile of v0, /device:TPU:1, one launch (start us, length us, event | category | flops | bytes accessed | tf_op | source)
XLA Modules:
  0.0 233.4 jit_solution(199019908861297292)
XLA Ops:
  0.0 0.0 copy-start.3
  0.0 3.2 %fusion.15 = (bf16[10,2,4,2,1536]{4,3,2,1,0:T(2,128)(2,1)S(1)}, bf16[10,2,4,2,1536]{4,3,2,1,0:T(2,128)(2,1)S(1)}) fusion(bf16[10,2,4,8,1536]{4,3,2,1,0:T(8,128)(2,1)} %param.5), kind=kLoop, calls=%fused_computation.46 | loop fusion | bytes 1966080 | tf_op jit(solution)/shard_map/slice | solution.py:15
  3.3 0.2 copy.164
  3.5 3.3 %collective-permute-start = (bf16[10,2,4,2,1536]{4,2,3,1,0:T(4,128)(2,1)S(1)}, bf16[10,2,4,2,1536]{4,2,3,1,0:T(4,128)(2,1)S(1)}, u32[]{:S(2)}, u32[]{:S(2)}) collective-permute-start(bf16[10,2,4,2,1536]{4,2,3,1,0:T(4,128)(2,1)S(1)} %copy.164), channel_id=1, source_target_pairs={{1,0},{3,2},{5,4},{7,6},{9,8},{11,10},{13,12},{15,14},{17,16},{19,... | collective-permute-start | bytes 1474568 | tf_op jit(solution)/shard_map/ppermute | solution.py:15
  6.8 0.2 copy.165
  7.0 1.3 collective-permute-start.1
  8.4 1.5 constant_dynamic-update-slice_fusion
  10.0 0.1 fusion.10
  10.1 0.0 copy-done.3
  10.2 0.1 compare_convert_fusion
  10.2 0.7 collective-permute-done.1
  10.9 1.4 copy.148
  12.4 0.0 collective-permute-done
  12.4 1.3 copy_dynamic-update-slice_fusion
  13.7 5.9 %add_multiply_fusion = f32[10,2,4,8,1536]{4,3,2,1,0:T(8,128)S(1)} fusion(bf16[10,2,4,8,1536]{4,3,2,1,0:T(8,128)(2,1)S(1)} %copy-done, bf16[10,2,4,2,1536]{4,3,2,1,0:T(2,128)(2,1)S(1)} %copy.148, bf16[10,2,4,10,1536]{4,3,2,1,0:T(8,128)(2,1)} %copy_dynamic-update-slice_fusion, f32[10,1536]{1,0:T(8,128)S(1)} %compare_convert_fusion, ...), kind=kLoop, calls=%fused_computation.9 | loop fusion | flops 20643840 | bytes 10384000 | tf_op jit(solution)/shard_map/mul | solution.py:60
  19.6 0.3 slice_add_fusion
  19.9 2.2 pad_maximum_fusion
  22.2 26.9 %copy.149 = f32[10,2,4,8,1536]{0,3,4,2,1:T(8,128)} copy(f32[10,2,4,8,1536]{4,3,2,1,0:T(8,128)} %pad_maximum_fusion) | data formatting | bytes 7864320 | tf_op jit(solution)/shard_map/stack | solution.py:61
  49.1 39.0 %gather_fusion = f32[1536,10,2,4,8]{1,4,3,2,0:T(8,128)} fusion(f32[10,2,4,8,1536]{0,3,4,2,1:T(8,128)} %copy.149, s32[2048]{0:T(1024)S(1)} %pad_clamp_fusion), kind=kCustom, calls=%fused_computation | custom fusion | bytes 7870464 | tf_op jit(solution)/shard_map/jit(_take)/gather | solution.py:63
  88.1 34.9 %copy.150 = f32[10,2,4,8,2,768]{5,1,4,3,2,0:T(2,128)} copy(f32[10,2,4,8,2,768]{0,3,2,1,5,4:T(8,128)} %bitcast.36) | data formatting | bytes 7864320 | tf_op jit(solution)/shard_map/jit(_take)/gather | solution.py:63
  123.1 7.5 %broadcast_select_fusion = f32[10,2,4,8,2,768]{5,1,4,3,2,0:T(2,128)} fusion(f32[10,2,4,8,2,768]{5,1,4,3,2,0:T(2,128)} %copy.150, pred[2,768]{1,0:T(4,128)(4,1)S(1)} %compare_and_fusion), kind=kLoop, calls=%fused_computation.10 | loop fusion | flops 983040 | bytes 7865856 | tf_op jit(solution)/shard_map/jit(_take)/select_n | solution.py:63
  130.5 8.1 %copy.151 = f32[768,2,640]{2,1,0:T(2,128)} copy(f32[768,2,640]{0,1,2:T(2,128)} %bitcast.38) | data formatting | bytes 7864320 | tf_op jit(solution)/shard_map/reshape | solution.py:65
  138.6 11.7 %all-to-all-start = ((f32[768,2,640]{2,1,0:T(2,128)}), f32[768,2,640]{2,1,0:T(2,128)}, u32[]{:S(2)}, u32[]{:S(2)}) async-start(f32[768,2,640]{2,1,0:T(2,128)} %copy.151), calls=%async_computation | async-start | bytes 7864320 | tf_op jit(solution)/shard_map/all_to_all | solution.py:68
  150.3 29.5 %copy.153 = bf16[6,2,640,640]{2,1,3,0:T(2,128)(2,1)} copy(bf16[6,2,640,640]{3,2,1,0:T(8,128)(2,1)} %param.8) | data formatting | bytes 19660800 | tf_op args[3]
  179.8 0.1 dynamic_slice.18
  179.9 0.1 broadcast_add_fusion
  180.0 20.4 %all-to-all-done = f32[768,2,640]{2,1,0:T(2,128)} async-done(((f32[768,2,640]{2,1,0:T(2,128)}), f32[768,2,640]{2,1,0:T(2,128)}, u32[]{:S(2)}, u32[]{:S(2)}) %all-to-all-start) | async-done | bytes 3932192 | tf_op jit(solution)/shard_map/all_to_all | solution.py:68
  200.4 9.9 %reshape.212 = f32[6,2,64,2,10,64]{5,4,1,0,3,2:T(8,128)} reshape(f32[6,2,128,640]{3,1,0,2:T(2,128)} %bitcast.10) | data formatting | bytes 7864320 | tf_op jit(solution)/shard_map/reshape | solution.py:69
  210.3 20.1 %fusion = bf16[6,2,2,64,640,1]{4,3,5,2,1,0:T(8,128)(2,1)S(1)} fusion(bf16[6,2,640,64,10,1]{2,1,4,3,0,5:T(2,128)(2,1)} %bitcast.37, f32[6,2,64,2,10,64]{5,4,1,0,3,2:T(8,128)} %reshape.212), kind=kOutput, calls=%fused_computation.1 | convolution fusion | flops 7549747200 | bytes 15728640 | tf_op jit(solution)/shard_map/qskap,qsavpc->qskvc/dot_general | solution.py:78
  230.4 0.2 copy.156
  230.6 0.6 fusion.3
  231.1 2.3 copy.157
  (17 shorter events, 0.1 us)
Async XLA Ops:
  0.0 8.3 %copy-start = (bf16[10,2,4,8,1536]{4,3,2,1,0:T(8,128)(2,1)S(1)}, bf16[10,2,4,8,1536]{4,3,2,1,0:T(8,128)(2,1)}, u32[]{:S(2)}) copy-start(bf16[10,2,4,8,1536]{4,3,2,1,0:T(8,128)(2,1)} %param.5) | copy-start | bytes 5898244
  0.0 9.9 %copy-start.1 = (s32[768]{0:T(1024)S(1)}, s32[768]{0:T(1024)}, u32[]{:S(2)}) copy-start(s32[768]{0:T(1024)} %param.9) | copy-start | bytes 9220
  0.0 10.0 %copy-start.2 = (f32[4,16,5]{1,0,2:T(4,128)S(1)}, f32[4,16,5]{1,0,2:T(4,128)}, u32[]{:S(2)}) copy-start(f32[4,16,5]{1,0,2:T(4,128)} %param.6) | copy-start | bytes 3844
  0.0 10.1 %copy-start.3 = (s32[10]{0:T(128)S(1)}, s32[10]{0:T(128)}, u32[]{:S(2)}) copy-start(s32[10]{0:T(128)} %param.7) | copy-start | bytes 124
  3.5 8.9 %collective-permute-start = (bf16[10,2,4,2,1536]{4,2,3,1,0:T(4,128)(2,1)S(1)}, bf16[10,2,4,2,1536]{4,2,3,1,0:T(4,128)(2,1)S(1)}, u32[]{:S(2)}, u32[]{:S(2)}) collective-permute-start(bf16[10,2,4,2,1536]{4,2,3,1,0:T(4,128)(2,1)S(1)} %copy.164), channel_id=1, source_target_pairs={{1,0},{3,2},{5,4},{7,6},{9,8},{11,10},{13,12},{15,14},{17,16},{19,... | collective-permute-start | bytes 1474568 | tf_op jit(solution)/shard_map/ppermute | solution.py:15
  7.0 3.9 %collective-permute-start.1 = (bf16[10,2,4,2,1536]{4,2,3,1,0:T(4,128)(2,1)S(1)}, bf16[10,2,4,2,1536]{4,2,3,1,0:T(4,128)(2,1)}, u32[]{:S(2)}, u32[]{:S(2)}) collective-permute-start(bf16[10,2,4,2,1536]{4,2,3,1,0:T(4,128)(2,1)S(1)} %copy.165), channel_id=1, source_target_pairs={{0,1},{2,3},{4,5},{6,7},{8,9},{10,11},{12,13},{14,15},{16,17},{18,... | collective-permute-start | bytes 1474568 | tf_op jit(solution)/shard_map/ppermute | solution.py:12
  138.6 61.7 %all-to-all-start = ((f32[768,2,640]{2,1,0:T(2,128)}), f32[768,2,640]{2,1,0:T(2,128)}, u32[]{:S(2)}, u32[]{:S(2)}) async-start(f32[768,2,640]{2,1,0:T(2,128)} %copy.151), calls=%async_computation | async-start | bytes 7864320 | tf_op jit(solution)/shard_map/all_to_all | solution.py:68
where the time goes:
time: 236 us; the launch traced here: 233 us
  local copies, waits for them, and re-layouts  159 us (67%)
  waiting for transfers between devices  21.1 us (9%)
  matrix products  20.1 us (9%)
  other arithmetic  16.8 us (7%)
  starting transfers between devices  16.3 us (7%)
    gather x2, local copies, waits for them, and re-layouts, body(): ordered = jnp.take(folded, picked, axis=4)  74 us
    unnamed x13, local copies, waits for them, and re-layouts  31.4 us
    another operation x1, local copies, waits for them, and re-layouts, body(): jnp.stack([masked[:, 0] + masked[:, 1], masked[:, 0] - masked[:, 1]], axi...  26.9 us
    all_to_all x1, waiting for transfers between devices, body(): lax.all_to_all(outgoing, ('lat', 'lev'), split_axis=0, concat_axis=2, til...  20.4 us
    dot_general x1, matrix products, body(): jnp.einsum('q' + form.replace(',', ',q').replace('->', '->q'), table_all....  20.1 us
    all_to_all x1, starting transfers between devices, body(): lax.all_to_all(outgoing, ('lat', 'lev'), split_axis=0, concat_axis=2, til...  11.7 us
    reshape x1, local copies, waits for them, and re-layouts, body(): arrived.reshape(slots_here, 2, lat_count, lev_count, pairs_here, fields *...  9.91 us
    reshape x1, local copies, waits for them, and re-layouts, body(): jnp.transpose(split, (5, 1, 0, 2, 3, 4))  8.09 us
  transfers between devices with their start and end apart: 3, of which 2 were waited for; matrix products, arithmetic and copies ran while one was open for 14% of the time, Pallas kernels for 0%

commit v1 on v0

v1 whole, which is shorter than its diff:
```python
import functools

import jax
import jax.numpy as jnp
import numpy as np
from jax import lax
from jax.experimental import pallas as pl
from jax.experimental.pallas import tpu as pltpu
from jax.sharding import PartitionSpec as P

NT_DIMS = (((1,), (1,)), ((), ()))


def pack_kernel(fourier_ref, cycles_ref, wave_ref, out_ref, pick_ref, column_ref, rows_ref, *, lev, slots):
    pairs, parts, waves = fourier_ref.shape[0], 2, fourier_ref.shape[2] // 2
    holders = waves // slots
    lat = holders // lev
    for i in range(waves // 128):
        line = jnp.broadcast_to(wave_ref[pl.ds(i, 1), :], (128, 128))
        column_ref[pl.ds(i * 128, 128), :] = line.T
    lane = lax.broadcasted_iota(jnp.int32, (lat, 128), 1)
    for q in range(slots):
        for v in range(lev):
            column = column_ref[pl.ds(v * slots + q, lat, stride=lev * slots), :]
            for b in range(waves // 128):
                hit = jnp.where(column == lane + b * 128, 1.0, 0.0).astype(jnp.bfloat16)
                pick_ref[pl.ds((q * lev + v) * lat, lat), pl.ds(b * 128, 128)] = hit
    wave = lax.broadcasted_iota(jnp.int32, (1, waves), 1)
    run = pairs * slots
    for j in range(0, pairs, 2):
        blocks = []
        for i in (j, j + 1):
            keep = 2 * wave < cycles_ref[i]
            for r in range(parts):
                part = fourier_ref[i, :, pl.ds(r * waves, waves)]
                blocks.append(jnp.where(keep, part, jnp.zeros_like(part)))
        block = jnp.concatenate(blocks, axis=0)
        for q in range(slots):
            picked = lax.dot_general(
                pick_ref[pl.ds(q * holders, holders), :], block, NT_DIMS,
                preferred_element_type=jnp.float32,
            )
            for i in range(2):
                rows_ref[pl.ds((j + i) * slots + q, holders, stride=run), :] = picked[:, i * 128:(i + 1) * 128]
    out_ref[...] = rows_ref[...].astype(jnp.bfloat16)


def split_bf16(value):
    high = value.astype(jnp.bfloat16)
    low = (value - high.astype(jnp.float32)).astype(jnp.bfloat16)
    return high, low


def transform_kernel(wave_ref, arrived_ref, vertical_ref, table_ref, out_ref,
                     arrived, tables, folded, result, arrived_sem, table_sem, out_sem, *, lev, limit):
    slots, sides, rows, pairs = tables.shape
    half = arrived.shape[0] // lev
    arrive = pltpu.make_async_copy(arrived_ref, arrived, arrived_sem)
    arrive.start()
    for q in range(slots):
        for s in range(sides):
            pltpu.make_async_copy(table_ref.at[q, s], tables.at[q, s], table_sem.at[q, s]).start()
    v_high, v_low = split_bf16(vertical_ref[...])
    arrive.wait()
    step = 480

    @pl.loop(0, half // step)
    def _(i):
        at = pl.multiple_of(i * step, step)
        source = jnp.concatenate([arrived[pl.ds(v * half + at, step), :] for v in range(lev)], axis=1)
        made = jnp.dot(source, v_high, preferred_element_type=jnp.float32)
        made = made + jnp.dot(source, v_low, preferred_element_type=jnp.float32)
        for s in range(sides):
            folded[s, pl.ds(at, step), :] = made[:, s * 128:(s + 1) * 128]

    degree = 2 * lax.broadcasted_iota(jnp.int32, (rows, 128), 0)

    @pl.loop(0, slots)
    def _(q):
        for s in range(sides):
            column = folded[s, pl.ds(q, pairs, stride=slots), :]
            right = jnp.concatenate(split_bf16(column), axis=1)
            pltpu.make_async_copy(table_ref.at[q, s], tables.at[q, s], table_sem.at[q, s]).wait()
            both = jnp.dot(tables[q, s], right, preferred_element_type=jnp.float32)
            product = both[:, :128] + both[:, 128:]
            valid = degree < limit - s - wave_ref[q]
            result[q, s] = jnp.where(valid, product, 0.0).astype(jnp.bfloat16)
            pltpu.make_async_copy(result.at[q, s], out_ref.at[q, s], out_sem.at[q, s]).start()

    for q in range(slots):
        for s in range(sides):
            pltpu.make_async_copy(result.at[q, s], out_ref.at[q, s], out_sem.at[q, s]).wait()


def vertical_matrix(band, lev):
    fields, levels, width = band.shape
    reach = (width - 1) // 2
    here = levels // lev
    source = band.reshape(fields, lev, here, width).transpose(1, 0, 2, 3)[:, None, None]
    source = jnp.broadcast_to(source, (lev, 2, 2, fields, here, width)).reshape(-1, width)
    row = np.arange(source.shape[0])[:, None]
    column = np.arange(source.shape[0])[None, :]
    row_level = row // (4 * fields * here) * here + row % here
    row_group = row // (2 * fields * here) % 2 * fields + row // here % fields
    group = column % 2 * fields + column // (2 * levels) % fields
    offset = np.where(row_group == group, column // 2 % levels - row_level + reach, width).astype(np.int8)
    sign = np.where((row // (here * fields) % 2 == 1) & (column // (2 * levels * fields) == 1), -1, 1).astype(np.int8)
    value = jnp.zeros(offset.shape, jnp.float32)
    for d in range(width):
        value = jnp.where(offset == d, source[:, d:d + 1], value)
    return value * sign


def pack(fourier, cycle_points, wave_of_slot, lev, slots):
    pairs, sides, fields, here, columns = fourier.shape
    waves = columns // 2
    holders = waves // slots
    lanes = sides * fields * here
    return pl.pallas_call(
        functools.partial(pack_kernel, lev=lev, slots=slots),
        out_shape=jax.ShapeDtypeStruct((waves * pairs, 2 * lanes), jnp.bfloat16),
        in_specs=[
            pl.BlockSpec(memory_space=pltpu.VMEM),
            pl.BlockSpec(memory_space=pltpu.SMEM),
            pl.BlockSpec(memory_space=pltpu.VMEM),
        ],
        out_specs=pl.BlockSpec(memory_space=pltpu.VMEM),
        scratch_shapes=[
            pltpu.VMEM((waves, waves), jnp.bfloat16),
            pltpu.VMEM((waves, 128), jnp.int32),
            pltpu.VMEM((waves * pairs, 2 * lanes), jnp.float32),
        ],
        compiler_params=pltpu.CompilerParams(vmem_limit_bytes=40 * 1024 * 1024),
        name="pack",
    )(fourier.reshape(pairs, lanes, columns), cycle_points, wave_of_slot.reshape(waves // 128, 128))


def transform(own_waves, arrived, vertical, legendre, lev):
    slots, sides, rows, pairs = legendre.shape
    total, lanes = arrived.shape
    any_space = pl.BlockSpec(memory_space=pl.ANY)
    return pl.pallas_call(
        functools.partial(transform_kernel, lev=lev, limit=2 * rows),
        out_shape=jax.ShapeDtypeStruct((slots, sides, rows, lanes), jnp.bfloat16),
        in_specs=[
            pl.BlockSpec(memory_space=pltpu.SMEM),
            any_space,
            pl.BlockSpec(memory_space=pltpu.VMEM),
            any_space,
        ],
        out_specs=any_space,
        scratch_shapes=[
            pltpu.VMEM((total, lanes), jnp.bfloat16),
            pltpu.VMEM((slots, sides, rows, pairs), jnp.bfloat16),
            pltpu.VMEM((sides, total // lev, lanes), jnp.float32),
            pltpu.VMEM((slots, sides, rows, lanes), jnp.bfloat16),
            pltpu.SemaphoreType.DMA,
            pltpu.SemaphoreType.DMA((slots, sides)),
            pltpu.SemaphoreType.DMA((slots, sides)),
        ],
        compiler_params=pltpu.CompilerParams(vmem_limit_bytes=40 * 1024 * 1024),
        name="transform",
    )(own_waves, arrived, vertical, legendre)


def body(fourier, vertical_band, cycle_points, legendre, wave_of_slot):
    slots = legendre.shape[0]
    lat, lev = lax.axis_size("lat"), lax.axis_size("lev")
    outgoing = pack(fourier, cycle_points, wave_of_slot, lev, slots)
    split = outgoing.reshape(lat * lev, outgoing.shape[0] // (lat * lev * 4), 4, outgoing.shape[1])
    arrived = lax.all_to_all(split, ("lev", "lat"), split_axis=0, concat_axis=0, tiled=True)
    vertical_band, waves = lax.optimization_barrier((vertical_band, wave_of_slot, outgoing))[:2]
    own_waves = lax.dynamic_slice_in_dim(waves, lax.axis_index(("lat", "lev")) * slots, slots)
    vertical = vertical_matrix(vertical_band, lev)
    return transform(own_waves, arrived.reshape(outgoing.shape), vertical, legendre, lev)


def solution(mesh):
    in_specs = (
        P("lat", None, None, "lev", None),
        P(),
        P("lat"),
        P(("lat", "lev"), None, None, None),
        P(),
    )
    out_specs = P(("lat", "lev"), None, None, None)
    return jax.shard_map(body, mesh=mesh, in_specs=in_specs, out_specs=out_specs, check_vma=False)
```

time: 236 us -> 65.6 us (0.28)
  local copies, waits for them, and re-layouts: 159 us -> 7.71 us
  matrix products: 20.1 us -> 0 us
  Pallas kernels: 0 us -> 19.6 us
  other arithmetic: 16.8 us -> 0.24 us
  starting transfers between devices: 16.3 us -> 11.5 us
  waiting for transfers between devices: 21.1 us -> 25.8 us
    gather x2 -> x0, local copies, waits for them, and re-layouts: 74 us -> none  [body(): ordered = jnp.take(folded, picked, axis=4)]
    another operation x1 -> x0, local copies, waits for them, and re-layouts: 26.9 us -> none  [body(): jnp.stack([masked[:, 0] + masked[:, 1], masked[:, 0] - masked[:, 1]], axi...]
    unnamed x13 -> x22, local copies, waits for them, and re-layouts: 31.4 us -> 6.71 us
    dot_general x1 -> x0, matrix products: 20.1 us -> none  [body(): jnp.einsum('q' + form.replace(',', ',q').replace('->', '->q'), table_all....]
    pallas_call x0 -> x2, Pallas kernels: none -> 19.6 us  [the longest x1 13.6 us: transform(): pl.pallas_call(functools.partial(transform_kernel, lev=lev, limit=2 * row...]
    reshape x3 -> x2, local copies, waits for them, and re-layouts: 18.2 us -> 0.2 us  [the longest x1 0.12 us: vertical_matrix(): jnp.broadcast_to(source, (lev, 2, 2, fields, here, width))]
    select_n x2 -> x0, other arithmetic: 7.5 us -> none  [body(): ordered = jnp.take(folded, picked, axis=4)]
    mul x3 -> x1, other arithmetic: 5.92 us -> 0.24 us  [vertical_matrix(): return value * sign]
  transfers between devices with their start and end apart: 3 -> 1, of which waited for: 2 -> 1; matrix products, arithmetic and copies ran while one was open for 14% -> 2% of each run, Pallas kernels for 0% -> 0%
where the time goes in v1:
time: 65.6 us; the launch traced here: 64.9 us
  waiting for transfers between devices  25.8 us (39%)
  Pallas kernels  19.6 us (30%)
  starting transfers between devices  11.5 us (18%)
  local copies, waits for them, and re-layouts  7.71 us (12%)
    all_to_all x1, waiting for transfers between devices, body(): lax.all_to_all(split, ('lev', 'lat'), split_axis=0, concat_axis=0, tiled=...  25.8 us
    pallas_call x1, Pallas kernels, transform(): pl.pallas_call(functools.partial(transform_kernel, lev=lev, limit=2 * row...  13.6 us
    all_to_all x1, starting transfers between devices, body(): lax.all_to_all(split, ('lev', 'lat'), split_axis=0, concat_axis=0, tiled=...  11.5 us
    unnamed x22, local copies, waits for them, and re-layouts  6.71 us
    pallas_call x1, Pallas kernels, pack(): pl.pallas_call(functools.partial(pack_kernel, lev=lev, slots=slots), out_...  6 us
  transfers between devices with their start and end apart: 1, of which 1 were waited for; matrix products, arithmetic and copies ran while one was open for 2% of the time, Pallas kernels for 0%

profile of v1, /device:TPU:1, one launch (start us, length us, event | category | flops | bytes accessed | tf_op | source)
XLA Modules:
  0.0 64.9 jit_solution(14623272700827155581)
XLA Ops:
  0.0 0.0 copy-start.1
  0.0 1.5 %copy-done.1 = bf16[10,2,4,8,1536]{4,3,2,1,0:T(8,128)(2,1)S(1)} copy-done((bf16[10,2,4,8,1536]{4,3,2,1,0:T(8,128)(2,1)S(1)}, bf16[10,2,4,8,1536]{4,3,2,1,0:T(8,128)(2,1)}, u32[]{:S(2)}) %copy-start.1) | copy-done | bytes 1966104
  1.5 0.0 copy-start.2
  1.5 0.7 %copy-done.2 = s32[768]{0:T(1024)S(1)} copy-done((s32[768]{0:T(1024)S(1)}, s32[768]{0:T(1024)}, u32[]{:S(2)}) %copy-start.2) | copy-done | bytes 3096
  2.2 0.0 copy-start.3
  2.2 0.7 %copy-done.3 = s32[10]{0:T(128)S(1)} copy-done((s32[10]{0:T(128)S(1)}, s32[10]{0:T(128)}, u32[]{:S(2)}) %copy-start.3) | copy-done | bytes 64
  2.9 6.0 %pack.1 = bf16[7680,128]{1,0:T(8,128)(2,1)} custom-call(bf16[10,64,1536]{2,1,0:T(8,128)(2,1)S(1)} %bitcast.15, s32[10]{0:T(128)S(1)} %copy-done.3, s32[6,128]{1,0:T(8,128)S(1)} %bitcast.16), custom_call_target="tpu_custom_call" | custom-call | tf_op jit(solution)/shard_map/pack/pallas_call | solution.py:119
  8.9 0.0 copy-start.10
  8.9 0.0 copy-start.4
  8.9 0.0 copy-start.5
  8.9 0.0 copy-start.6
  8.9 0.0 copy-start.7
  8.9 0.0 copy-start.8
  8.9 0.0 copy-start.9
  8.9 11.5 %all-to-all-start = ((bf16[128,15,4,128]{3,2,1,0:T(4,128)(2,1)}), bf16[128,15,4,128]{3,2,1,0:T(4,128)(2,1)S(1)}, u32[]{:S(2)}, u32[]{:S(2)}) async-start(bf16[128,15,4,128]{3,2,1,0:T(4,128)(2,1)} %bitcast.2), calls=%async_computation | async-start | bytes 3932160 | tf_op jit(solution)/shard_map/all_to_all | solution.py:171
  20.5 0.0 copy-done.10
  20.5 0.1 reshape.23
  20.6 0.1 reshape.24
  20.7 0.8 %dynamic_slice.3.wave_ref = s32[6]{0:T(128)S(1)} dynamic-slice(s32[768]{0:T(1024)} %param.15, s32[]{:T(128)S(6)} %select_n.19), dynamic_slice_sizes={6} | dynamic-slice | bytes 52 | tf_op jit(solution)/shard_map/dynamic_slice | solution.py:173
  21.5 0.0 copy-done.4
  21.5 0.0 copy-done.5
  21.5 0.0 copy-done.6
  21.5 0.0 copy-done.7
  21.5 0.0 copy-done.8
  21.5 0.0 copy-done.9
  21.5 0.2 select_multiply_fusion.vertical_ref
  21.8 25.8 %all-to-all-done = bf16[128,15,4,128]{3,2,1,0:T(4,128)(2,1)S(1)} async-done(((bf16[128,15,4,128]{3,2,1,0:T(4,128)(2,1)}), bf16[128,15,4,128]{3,2,1,0:T(4,128)(2,1)S(1)}, u32[]{:S(2)}, u32[]{:S(2)}) %all-to-all-start) | async-done | bytes 1966112 | tf_op jit(solution)/shard_map/all_to_all | solution.py:171
  47.6 0.0 copy-start
  47.6 3.8 %copy-done = bf16[6,2,640,640]{3,2,1,0:T(8,128)(2,1)S(1)} copy-done((bf16[6,2,640,640]{3,2,1,0:T(8,128)(2,1)S(1)}, bf16[6,2,640,640]{3,2,1,0:T(8,128)(2,1)}, u32[]{:S(2)}) %copy-start) | copy-done | bytes 9830424
  51.4 13.6 %transform.1 = bf16[6,2,640,128]{3,2,1,0:T(8,128)(2,1)} custom-call(s32[6]{0:T(128)S(1)} %dynamic_slice.3.wave_ref, bf16[7680,128]{1,0:T(8,128)(2,1)S(1)} %bitcast.14, f32[256,256]{1,0:T(8,128)S(1)} %select_multiply_fusion.vertical_ref, bf16[6,2,640,640]{3,2,1,0:T(8,128)(2,1)S(1)} %copy-done), custom_call_target="tpu_custom_call" | custom-call | tf_op jit(solution)/shard_map/transform/pallas_call | solution.py:142
  (3 shorter events, 0.0 us)
Async XLA Ops:
  0.0 1.5 %copy-start.1 = (bf16[10,2,4,8,1536]{4,3,2,1,0:T(8,128)(2,1)S(1)}, bf16[10,2,4,8,1536]{4,3,2,1,0:T(8,128)(2,1)}, u32[]{:S(2)}) copy-start(bf16[10,2,4,8,1536]{4,3,2,1,0:T(8,128)(2,1)} %param.11) | copy-start | bytes 5898244
  1.5 0.7 %copy-start.2 = (s32[768]{0:T(1024)S(1)}, s32[768]{0:T(1024)}, u32[]{:S(2)}) copy-start(s32[768]{0:T(1024)} %param.15) | copy-start | bytes 9220
  2.2 0.7 %copy-start.3 = (s32[10]{0:T(128)S(1)}, s32[10]{0:T(128)}, u32[]{:S(2)}) copy-start(s32[10]{0:T(128)} %cycles_ref.1) | copy-start | bytes 124
  8.9 11.6 %copy-start.10 = (f32[4,16,5]{1,0,2:T(4,128)S(1)}, f32[4,16,5]{1,0,2:T(4,128)}, u32[]{:S(2)}) copy-start(f32[4,16,5]{1,0,2:T(4,128)} %param.12) | copy-start | bytes 3844
  8.9 12.6 %copy-start.4 = (f32[256,256]{1,0:T(8,128)S(1)}, f32[256,256]{1,0:T(8,128)}, u32[]{:S(2)}) copy-start(f32[256,256]{1,0:T(8,128)} %constant.39) | copy-start | bytes 786436
  8.9 12.6 %copy-start.5 = (pred[256,256]{1,0:T(32,128)(4,1)S(1)}, pred[256,256]{1,0:T(32,128)(4,1)}, u32[]{:S(2)}) copy-start(pred[256,256]{1,0:T(32,128)(4,1)} %constant.34.clone) | copy-start | bytes 196612
  8.9 12.6 %copy-start.6 = (pred[256,256]{1,0:T(32,128)(4,1)S(1)}, pred[256,256]{1,0:T(32,128)(4,1)}, u32[]{:S(2)}) copy-start(pred[256,256]{1,0:T(32,128)(4,1)} %constant.33.clone) | copy-start | bytes 196612
  8.9 12.6 %copy-start.7 = (pred[256,256]{1,0:T(32,128)(4,1)S(1)}, pred[256,256]{1,0:T(32,128)(4,1)}, u32[]{:S(2)}) copy-start(pred[256,256]{1,0:T(32,128)(4,1)} %constant.32.clone) | copy-start | bytes 196612
  8.9 12.6 %copy-start.8 = (pred[256,256]{1,0:T(32,128)(4,1)S(1)}, pred[256,256]{1,0:T(32,128)(4,1)}, u32[]{:S(2)}) copy-start(pred[256,256]{1,0:T(32,128)(4,1)} %constant.31.clone) | copy-start | bytes 196612
  8.9 12.6 %copy-start.9 = (pred[256,256]{1,0:T(32,128)(4,1)S(1)}, pred[256,256]{1,0:T(32,128)(4,1)}, u32[]{:S(2)}) copy-start(pred[256,256]{1,0:T(32,128)(4,1)} %constant.30.clone) | copy-start | bytes 196612
  8.9 38.7 %all-to-all-start = ((bf16[128,15,4,128]{3,2,1,0:T(4,128)(2,1)}), bf16[128,15,4,128]{3,2,1,0:T(4,128)(2,1)S(1)}, u32[]{:S(2)}, u32[]{:S(2)}) async-start(bf16[128,15,4,128]{3,2,1,0:T(4,128)(2,1)} %bitcast.2), calls=%async_computation | async-start | bytes 3932160 | tf_op jit(solution)/shard_map/all_to_all | solution.py:171
  47.6 3.8 %copy-start = (bf16[6,2,640,640]{3,2,1,0:T(8,128)(2,1)S(1)}, bf16[6,2,640,640]{3,2,1,0:T(8,128)(2,1)}, u32[]{:S(2)}) copy-start(bf16[6,2,640,640]{3,2,1,0:T(8,128)(2,1)} %table_ref.1) | copy-start | bytes 29491204

commit v2 on v1

v2 whole, which is shorter than its diff:
```python
import functools

import jax
import jax.numpy as jnp
import numpy as np
from jax import lax
from jax.experimental import pallas as pl
from jax.experimental.pallas import tpu as pltpu
from jax.sharding import PartitionSpec as P

NT_DIMS = (((1,), (1,)), ((), ()))


def pack_kernel(cycles_ref, fourier_ref, wave_ref, out_ref,
                fourier, wave, pick, column_ref, rows_ref, packed, in_sem, wave_sem, out_sem, *, lev, slots):
    pairs, parts, waves = fourier_ref.shape[0], 2, fourier_ref.shape[2] // 2
    holders = waves // slots
    lat = holders // lev
    run = pairs * slots
    group = 2

    def arriving(j):
        return pltpu.make_async_copy(fourier_ref.at[pl.ds(j, group)], fourier.at[pl.ds(j, group)], in_sem.at[j // group])

    arrive_wave = pltpu.make_async_copy(wave_ref, wave, wave_sem)
    arrive_wave.start()
    for j in range(0, pairs, group):
        arriving(j).start()
    arrive_wave.wait()
    shape = (waves // 128, 128)
    slot = lax.rem(lax.broadcasted_iota(jnp.int32, shape, 0) * 128 + lax.broadcasted_iota(jnp.int32, shape, 1), slots)
    dealt = jnp.max(jnp.abs(lax.shift_right_logical(wave[...], 7) - slot)) == 0
    for i in range(waves // 128):
        column_ref[pl.ds(i * 128, 128), :] = jnp.broadcast_to(wave[pl.ds(i, 1), :], (128, 128)).T
    lane = lax.broadcasted_iota(jnp.int32, (lat, 128), 1)

    def fill(blocks_of):
        for q in range(slots):
            for v in range(lev):
                column = column_ref[pl.ds(v * slots + q, lat, stride=lev * slots), :]
                for b in blocks_of(q):
                    hit = jnp.where(column == lane + b * 128, 1.0, 0.0).astype(jnp.bfloat16)
                    pick[pl.ds((q * lev + v) * lat, lat), pl.ds(b * 128, 128)] = hit

    index = lax.broadcasted_iota(jnp.int32, (1, waves), 1)

    def gather(columns_of):
        for j in range(0, pairs, group):
            arriving(j).wait()
            blocks = []
            for i in range(j, j + group):
                keep = 2 * index < cycles_ref[i]
                for r in range(parts):
                    part = fourier[i, :, pl.ds(r * waves, waves)]
                    blocks.append(jnp.where(keep, part, jnp.zeros_like(part)))
            block = jnp.concatenate(blocks, axis=0)
            for q in range(slots):
                first, last = columns_of(q)
                picked = lax.dot_general(
                    pick[pl.ds(q * holders, holders), first:last], block[:, first:last], NT_DIMS,
                    preferred_element_type=jnp.float32,
                )
                for i in range(group):
                    rows_ref[pl.ds((j + i) * slots + q, holders, stride=run), :] = picked[:, i * 128:(i + 1) * 128]

    @pl.when(dealt)
    def _():
        fill(lambda q: [q])
        gather(lambda q: (q * 128, (q + 1) * 128))

    @pl.when(jnp.logical_not(dealt))
    def _():
        fill(lambda q: range(waves // 128))
        gather(lambda q: (0, waves))

    chunks = out_sem.shape[0]
    step = packed.shape[0] // chunks

    def leaving(i):
        part = pl.ds(i * step, step)
        return pltpu.make_async_copy(packed.at[part], out_ref.at[part], out_sem.at[i])

    for i in range(chunks):
        packed[pl.ds(i * step, step), :] = rows_ref[pl.ds(i * step, step), :].astype(jnp.bfloat16)
        leaving(i).start()
    for i in range(chunks):
        leaving(i).wait()


def split_bf16(value):
    high = value.astype(jnp.bfloat16)
    low = (value - high.astype(jnp.float32)).astype(jnp.bfloat16)
    return high, low


def transform_kernel(wave_ref, arrived_ref, vertical_ref, table_ref, out_ref,
                     arrived, vertical, tables, folded, right, result, in_sem, vertical_sem, table_sem, out_sem,
                     *, lev, limit):
    slots, sides, rows, pairs = tables.shape
    half = arrived.shape[0] // lev
    chunks = in_sem.shape[0]
    step = half // chunks
    tile = 128
    counts = range(rows // tile // 2 + 1, rows // tile + 1)

    def arriving(i, v):
        part = pl.ds(v * half + i * step, step)
        return pltpu.make_async_copy(arrived_ref.at[part], arrived.at[part], in_sem.at[i, v])

    def table(q, n):
        part = pl.ds(0, n * tile)
        return pltpu.make_async_copy(table_ref.at[q, :, part], tables.at[q, :, part], table_sem.at[q])

    def count(q):
        return jnp.clip((limit - wave_ref[q] + 2 * tile - 1) // (2 * tile), counts[0], counts[-1])

    def start_table(q):
        for n in counts:
            @pl.when(count(q) == n)
            def _():
                table(q, n).start()

    upper = pltpu.make_async_copy(vertical_ref, vertical, vertical_sem)
    upper.start()
    for i in range(chunks):
        for v in range(lev):
            arriving(i, v).start()
    upper.wait()
    ready = 0
    sent = 0
    for i in range(chunks):
        while ready < min(chunks, i + chunks // 2):
            for v in range(lev):
                arriving(ready, v).wait()
            ready += 1
        while sent < slots * ready // chunks:
            start_table(sent)
            sent += 1
        at = i * step
        source = jnp.concatenate([arrived[pl.ds(v * half + at, step), :] for v in range(lev)] * 2, axis=1)
        made = jnp.dot(source, vertical[...], preferred_element_type=jnp.float32)
        for s in range(sides):
            folded[s, pl.ds(at, step), :] = made[:, s * 128:(s + 1) * 128]

    degree = 2 * lax.broadcasted_iota(jnp.int32, (tile, 128), 0)

    def prepare(q, s):
        column = folded[s, pl.ds(q, pairs, stride=slots), :]
        right[s][...] = jnp.concatenate(split_bf16(column), axis=1)

    prepare(0, 0)

    @pl.loop(0, slots)
    def _(q):
        for n in counts:
            @pl.when(count(q) == n)
            def _():
                table(q, n).wait()
                for s in range(sides):
                    prepare(q, 1) if s == 0 else prepare(jnp.minimum(q + 1, slots - 1), 0)
                    for i in range(n):
                        part = pl.ds(i * tile, tile)
                        both = jnp.dot(tables[q, s, part], right[s][...], preferred_element_type=jnp.float32)
                        product = both[:, :128] + both[:, 128:]
                        valid = degree < limit - 2 * i * tile - s - wave_ref[q]
                        result[q, s, part] = jnp.where(valid, product, 0.0).astype(jnp.bfloat16)
                    if n * tile < rows:
                        rest = pl.ds(n * tile, rows - n * tile)
                        result[q, s, rest] = jnp.zeros((rows - n * tile, 128), jnp.bfloat16)
        pltpu.make_async_copy(result.at[q], out_ref.at[q], out_sem.at[q]).start()

    for q in range(slots):
        pltpu.make_async_copy(result.at[q], out_ref.at[q], out_sem.at[q]).wait()


def vertical_matrix(band, lev):
    fields, levels, width = band.shape
    reach = (width - 1) // 2
    here = levels // lev
    source = band.reshape(fields, lev, here, width).transpose(1, 0, 2, 3)[:, None, None]
    source = jnp.broadcast_to(source, (lev, 2, 2, fields, here, width)).reshape(-1, width)
    row = np.arange(source.shape[0])[:, None]
    column = np.arange(source.shape[0])[None, :]
    row_level = row // (4 * fields * here) * here + row % here
    row_group = row // (2 * fields * here) % 2 * fields + row // here % fields
    group = column % 2 * fields + column // (2 * levels) % fields
    offset = np.where(row_group == group, column // 2 % levels - row_level + reach, width).astype(np.int8)
    sign = np.where((row // (here * fields) % 2 == 1) & (column // (2 * levels * fields) == 1), -1, 1).astype(np.int8)
    value = jnp.zeros(offset.shape, jnp.float32)
    for d in range(width):
        value = jnp.where(offset == d, source[:, d:d + 1], value)
    value = value * sign
    high = lax.reduce_precision(value, 8, 7)
    return jnp.concatenate([high, value - high], axis=0).astype(jnp.bfloat16)


def pack(fourier, cycle_points, wave_of_slot, lev, slots):
    pairs, sides, fields, here, columns = fourier.shape
    waves = columns // 2
    lanes = sides * fields * here
    any_space = pl.BlockSpec(memory_space=pl.ANY)
    return pl.pallas_call(
        functools.partial(pack_kernel, lev=lev, slots=slots),
        out_shape=jax.ShapeDtypeStruct((waves * pairs, 2 * lanes), jnp.bfloat16),
        in_specs=[pl.BlockSpec(memory_space=pltpu.SMEM), any_space, any_space],
        out_specs=any_space,
        scratch_shapes=[
            pltpu.VMEM((pairs, lanes, columns), jnp.bfloat16),
            pltpu.VMEM((waves // 128, 128), jnp.int32),
            pltpu.VMEM((waves, waves), jnp.bfloat16),
            pltpu.VMEM((waves, 128), jnp.int32),
            pltpu.VMEM((waves * pairs, 2 * lanes), jnp.float32),
            pltpu.VMEM((waves * pairs, 2 * lanes), jnp.bfloat16),
            pltpu.SemaphoreType.DMA((pairs // 2,)),
            pltpu.SemaphoreType.DMA,
            pltpu.SemaphoreType.DMA((4,)),
        ],
        compiler_params=pltpu.CompilerParams(vmem_limit_bytes=60 * 1024 * 1024),
        name="pack",
    )(cycle_points, fourier.reshape(pairs, lanes, columns), wave_of_slot.reshape(waves // 128, 128))


def transform(own_waves, arrived, vertical, legendre, lev):
    slots, sides, rows, pairs = legendre.shape
    total, lanes = arrived.shape
    any_space = pl.BlockSpec(memory_space=pl.ANY)
    return pl.pallas_call(
        functools.partial(transform_kernel, lev=lev, limit=2 * rows),
        out_shape=jax.ShapeDtypeStruct((slots, sides, rows, lanes), jnp.bfloat16),
        in_specs=[
            pl.BlockSpec(memory_space=pltpu.SMEM),
            any_space,
            any_space,
            any_space,
        ],
        out_specs=any_space,
        scratch_shapes=[
            pltpu.VMEM((total, lanes), jnp.bfloat16),
            pltpu.VMEM(vertical.shape, jnp.bfloat16),
            pltpu.VMEM((slots, sides, rows, pairs), jnp.bfloat16),
            pltpu.VMEM((sides, total // lev, lanes), jnp.float32),
            [pltpu.VMEM((pairs, 2 * lanes), jnp.bfloat16)] * sides,
            pltpu.VMEM((slots, sides, rows, lanes), jnp.bfloat16),
            pltpu.SemaphoreType.DMA((4, lev)),
            pltpu.SemaphoreType.DMA,
            pltpu.SemaphoreType.DMA((slots,)),
            pltpu.SemaphoreType.DMA((slots,)),
        ],
        compiler_params=pltpu.CompilerParams(vmem_limit_bytes=60 * 1024 * 1024),
        name="transform",
    )(own_waves, arrived, vertical, legendre)


def body(fourier, vertical_band, cycle_points, legendre, wave_of_slot):
    slots = legendre.shape[0]
    lat, lev = lax.axis_size("lat"), lax.axis_size("lev")
    outgoing = pack(fourier, cycle_points, wave_of_slot, lev, slots)
    split = outgoing.reshape(lat * lev, outgoing.shape[0] // (lat * lev * 4), 4, outgoing.shape[1])
    arrived = lax.all_to_all(split, ("lev", "lat"), split_axis=0, concat_axis=0, tiled=True)
    vertical_band, waves = lax.optimization_barrier((vertical_band, wave_of_slot, outgoing))[:2]
    own_waves = lax.dynamic_slice_in_dim(waves, lax.axis_index(("lat", "lev")) * slots, slots)
    vertical = vertical_matrix(vertical_band, lev)
    return transform(own_waves, arrived.reshape(outgoing.shape), vertical, legendre, lev)


def solution(mesh):
    in_specs = (
        P("lat", None, None, "lev", None),
        P(),
        P("lat"),
        P(("lat", "lev"), None, None, None),
        P(),
    )
    out_specs = P(("lat", "lev"), None, None, None)
    return jax.shard_map(body, mesh=mesh, in_specs=in_specs, out_specs=out_specs, check_vma=False)
```

time: 65.6 us -> 54.6 us (0.83)
  Pallas kernels: 19.6 us -> 13.9 us
  local copies, waits for them, and re-layouts: 7.71 us -> 2.92 us
  waiting for transfers between devices: 25.8 us -> 24.5 us
  other arithmetic: 0.24 us -> 0.98 us
    unnamed x22 -> x16, local copies, waits for them, and re-layouts: 6.71 us -> 1.34 us
    pallas_call x1, Pallas kernels: 13.6 us -> 9.06 us  [transform(): pl.pallas_call(functools.partial(transform_kernel, lev=lev, limit=2 * row...]
    all_to_all x1, waiting for transfers between devices: 25.8 us -> 24.5 us  [body(): lax.all_to_all(split, ('lev', 'lat'), split_axis=0, concat_axis=0, tiled=...]
    pallas_call x1, Pallas kernels: 6 us -> 4.88 us  [pack(): pl.pallas_call(functools.partial(pack_kernel, lev=lev, slots=slots), out_...]
    concatenate x0 -> x1, other arithmetic: none -> 0.74 us  [vertical_matrix(): return jnp.concatenate([high, value - high], axis=0).astype(jnp.bfloat16)]
  transfers between devices with their start and end apart: 1 -> 1, of which waited for: 1 -> 1; matrix products, arithmetic and copies ran while one was open for 2% -> 5% of each run, Pallas kernels for 0% -> 0%
where the time goes in v2:
time: 54.6 us; the launch traced here: 54 us
  waiting for transfers between devices  24.5 us (45%)
  Pallas kernels  13.9 us (25%)
  starting transfers between devices  11.5 us (21%)
  local copies, waits for them, and re-layouts  2.92 us (5%)
  other arithmetic  0.98 us (2%)
    all_to_all x1, waiting for transfers between devices, body(): lax.all_to_all(split, ('lev', 'lat'), split_axis=0, concat_axis=0, tiled=...  24.5 us
    all_to_all x1, starting transfers between devices, body(): lax.all_to_all(split, ('lev', 'lat'), split_axis=0, concat_axis=0, tiled=...  11.5 us
    pallas_call x1, Pallas kernels, transform(): pl.pallas_call(functools.partial(transform_kernel, lev=lev, limit=2 * row...  9.06 us
    pallas_call x1, Pallas kernels, pack(): pl.pallas_call(functools.partial(pack_kernel, lev=lev, slots=slots), out_...  4.88 us
    dynamic_slice x1, local copies, waits for them, and re-layouts, body(): lax.dynamic_slice_in_dim(waves, lax.axis_index(('lat', 'lev')) * slots, s...  1.35 us
    unnamed x16, local copies, waits for them, and re-layouts  1.34 us
  transfers between devices with their start and end apart: 1, of which 1 were waited for; matrix products, arithmetic and copies ran while one was open for 5% of the time, Pallas kernels for 0%

profile of v2, /device:TPU:1, one launch (start us, length us, event | category | flops | bytes accessed | tf_op | source)
XLA Modules:
  0.0 54.0 jit_solution(6711055541150961002)
XLA Ops:
  0.0 4.9 %pack.1 = bf16[7680,128]{1,0:T(8,128)(2,1)} custom-call(s32[10]{0:T(128)} %cycles_ref.1, bf16[10,64,1536]{2,1,0:T(8,128)(2,1)} %bitcast.16, s32[6,128]{1,0:T(8,128)} %bitcast.18), custom_call_target="tpu_custom_call" | custom-call | tf_op jit(solution)/shard_map/pack/pallas_call | solution.py:202
  4.9 0.0 copy-start.7
  4.9 0.0 copy-start.1
  4.9 0.0 copy-start.2
  4.9 0.0 copy-start.3
  4.9 0.0 copy-start.4
  5.0 0.0 copy-start.5
  5.0 0.0 copy-start.6
  5.0 11.5 %all-to-all-start = ((bf16[128,15,4,128]{3,2,1,0:T(4,128)(2,1)}), bf16[128,15,4,128]{3,2,1,0:T(4,128)(2,1)S(1)}, u32[]{:S(2)}, u32[]{:S(2)}) async-start(bf16[128,15,4,128]{3,2,1,0:T(4,128)(2,1)} %bitcast.14), calls=%async_computation | async-start | bytes 3932160 | tf_op jit(solution)/shard_map/all_to_all | solution.py:259
  16.5 0.0 copy-done.7
  16.5 0.1 reshape.23
  16.6 0.1 reshape.24
  16.7 1.3 %dynamic_slice.3.wave_ref = s32[6]{0:T(128)} dynamic-slice(s32[768]{0:T(1024)} %param.15, s32[]{:T(128)S(6)} %select_n.19), dynamic_slice_sizes={6} | dynamic-slice | bytes 52 | tf_op jit(solution)/shard_map/dynamic_slice | solution.py:261
  18.1 0.0 copy-done.1
  18.1 0.0 copy-done.2
  18.1 0.0 copy-done.3
  18.1 0.0 copy-done.4
  18.1 0.0 copy-done.5
  18.1 0.0 copy-done.6
  18.2 0.2 reduce-precision_convert_fusion
  18.4 0.7 %pad_maximum_fusion.vertical_ref = bf16[512,256]{1,0:T(8,128)(2,1)} fusion(bf16[256,256]{1,0:T(8,128)(2,1)S(1)} %get-tuple-element.10, bf16[256,256]{1,0:T(8,128)(2,1)S(1)} %get-tuple-element.9), kind=kLoop, calls=%fused_computation.3 | loop fusion | flops 524288 | bytes 524288 | tf_op jit(solution)/shard_map/concatenate | solution.py:194
  19.1 24.5 %all-to-all-done = bf16[128,15,4,128]{3,2,1,0:T(4,128)(2,1)S(1)} async-done(((bf16[128,15,4,128]{3,2,1,0:T(4,128)(2,1)}), bf16[128,15,4,128]{3,2,1,0:T(4,128)(2,1)S(1)}, u32[]{:S(2)}, u32[]{:S(2)}) %all-to-all-start) | async-done | bytes 1966112 | tf_op jit(solution)/shard_map/all_to_all | solution.py:259
  43.6 0.0 copy-start
  43.6 1.3 %copy-done = bf16[128,15,4,128]{3,2,1,0:T(4,128)(2,1)} copy-done((bf16[128,15,4,128]{3,2,1,0:T(4,128)(2,1)}, bf16[128,15,4,128]{3,2,1,0:T(4,128)(2,1)S(1)}, u32[]{:S(2)}) %copy-start) | copy-done | bytes 1966104
  44.9 9.1 %transform.1 = bf16[6,2,640,128]{3,2,1,0:T(8,128)(2,1)} custom-call(s32[6]{0:T(128)} %dynamic_slice.3.wave_ref, bf16[7680,128]{1,0:T(8,128)(2,1)} %bitcast.15, bf16[512,256]{1,0:T(8,128)(2,1)} %pad_maximum_fusion.vertical_ref, bf16[6,2,640,640]{3,2,1,0:T(8,128)(2,1)} %table_ref.1), custom_call_target="tpu_custom_call" | custom-call | tf_op jit(solution)/shard_map/transform/pallas_call | solution.py:227
  (3 shorter events, 0.0 us)
Async XLA Ops:
  4.9 11.6 %copy-start.7 = (f32[4,16,5]{1,0,2:T(4,128)S(1)}, f32[4,16,5]{1,0,2:T(4,128)}, u32[]{:S(2)}) copy-start(f32[4,16,5]{1,0,2:T(4,128)} %param.12) | copy-start | bytes 3844
  4.9 13.2 %copy-start.1 = (f32[256,256]{1,0:T(8,128)S(1)}, f32[256,256]{1,0:T(8,128)}, u32[]{:S(2)}) copy-start(f32[256,256]{1,0:T(8,128)} %constant.39) | copy-start | bytes 786436
  4.9 13.2 %copy-start.2 = (pred[256,256]{1,0:T(32,128)(4,1)S(1)}, pred[256,256]{1,0:T(32,128)(4,1)}, u32[]{:S(2)}) copy-start(pred[256,256]{1,0:T(32,128)(4,1)} %constant.34.clone) | copy-start | bytes 196612
  4.9 13.2 %copy-start.3 = (pred[256,256]{1,0:T(32,128)(4,1)S(1)}, pred[256,256]{1,0:T(32,128)(4,1)}, u32[]{:S(2)}) copy-start(pred[256,256]{1,0:T(32,128)(4,1)} %constant.33.clone) | copy-start | bytes 196612
  4.9 13.2 %copy-start.4 = (pred[256,256]{1,0:T(32,128)(4,1)S(1)}, pred[256,256]{1,0:T(32,128)(4,1)}, u32[]{:S(2)}) copy-start(pred[256,256]{1,0:T(32,128)(4,1)} %constant.32.clone) | copy-start | bytes 196612
  5.0 13.2 %copy-start.5 = (pred[256,256]{1,0:T(32,128)(4,1)S(1)}, pred[256,256]{1,0:T(32,128)(4,1)}, u32[]{:S(2)}) copy-start(pred[256,256]{1,0:T(32,128)(4,1)} %constant.31.clone) | copy-start | bytes 196612
  5.0 13.2 %copy-start.6 = (pred[256,256]{1,0:T(32,128)(4,1)S(1)}, pred[256,256]{1,0:T(32,128)(4,1)}, u32[]{:S(2)}) copy-start(pred[256,256]{1,0:T(32,128)(4,1)} %constant.30.clone) | copy-start | bytes 196612
  5.0 38.6 %all-to-all-start = ((bf16[128,15,4,128]{3,2,1,0:T(4,128)(2,1)}), bf16[128,15,4,128]{3,2,1,0:T(4,128)(2,1)S(1)}, u32[]{:S(2)}, u32[]{:S(2)}) async-start(bf16[128,15,4,128]{3,2,1,0:T(4,128)(2,1)} %bitcast.14), calls=%async_computation | async-start | bytes 3932160 | tf_op jit(solution)/shard_map/all_to_all | solution.py:259
  43.6 1.3 %copy-start = (bf16[128,15,4,128]{3,2,1,0:T(4,128)(2,1)}, bf16[128,15,4,128]{3,2,1,0:T(4,128)(2,1)S(1)}, u32[]{:S(2)}) copy-start(bf16[128,15,4,128]{3,2,1,0:T(4,128)(2,1)S(1)} %all-to-all-done) | copy-start | bytes 5898244

commit v3 on v2

--- a/solution.py
+++ b/solution.py
@@ -12,7 +12,7 @@
 
 
 def pack_kernel(cycles_ref, fourier_ref, wave_ref, out_ref,
-                fourier, wave, pick, column_ref, rows_ref, packed, in_sem, wave_sem, out_sem, *, lev, slots):
+                fourier, wave, pick, column_ref, rows_ref, in_sem, wave_sem, *, lev, slots):
     pairs, parts, waves = fourier_ref.shape[0], 2, fourier_ref.shape[2] // 2
     holders = waves // slots
     lat = holders // lev
@@ -73,18 +73,7 @@
         fill(lambda q: range(waves // 128))
         gather(lambda q: (0, waves))
 
-    chunks = out_sem.shape[0]
-    step = packed.shape[0] // chunks
-
-    def leaving(i):
-        part = pl.ds(i * step, step)
-        return pltpu.make_async_copy(packed.at[part], out_ref.at[part], out_sem.at[i])
-
-    for i in range(chunks):
-        packed[pl.ds(i * step, step), :] = rows_ref[pl.ds(i * step, step), :].astype(jnp.bfloat16)
-        leaving(i).start()
-    for i in range(chunks):
-        leaving(i).wait()
+    out_ref[...] = rows_ref[...].astype(jnp.bfloat16)
 
 
 def split_bf16(value):
@@ -93,19 +82,14 @@
     return high, low
 
 
-def transform_kernel(wave_ref, arrived_ref, vertical_ref, table_ref, out_ref,
-                     arrived, vertical, tables, folded, right, result, in_sem, vertical_sem, table_sem, out_sem,
-                     *, lev, limit):
+def transform_kernel(wave_ref, arrived, vertical, table_ref, out_ref,
+                     tables, folded, right, result, table_sem, out_sem, *, lev, limit):
     slots, sides, rows, pairs = tables.shape
     half = arrived.shape[0] // lev
-    chunks = in_sem.shape[0]
+    chunks = 4
     step = half // chunks
     tile = 128
     counts = range(rows // tile // 2 + 1, rows // tile + 1)
-
-    def arriving(i, v):
-        part = pl.ds(v * half + i * step, step)
-        return pltpu.make_async_copy(arrived_ref.at[part], arrived.at[part], in_sem.at[i, v])
 
     def table(q, n):
         part = pl.ds(0, n * tile)
@@ -120,22 +104,9 @@
             def _():
                 table(q, n).start()
 
-    upper = pltpu.make_async_copy(vertical_ref, vertical, vertical_sem)
-    upper.start()
+    for q in range(slots):
+        start_table(q)
     for i in range(chunks):
-        for v in range(lev):
-            arriving(i, v).start()
-    upper.wait()
-    ready = 0
-    sent = 0
-    for i in range(chunks):
-        while ready < min(chunks, i + chunks // 2):
-            for v in range(lev):
-                arriving(ready, v).wait()
-            ready += 1
-        while sent < slots * ready // chunks:
-            start_table(sent)
-            sent += 1
         at = i * step
         source = jnp.concatenate([arrived[pl.ds(v * half + at, step), :] for v in range(lev)] * 2, axis=1)
         made = jnp.dot(source, vertical[...], preferred_element_type=jnp.float32)
@@ -203,17 +174,15 @@
         functools.partial(pack_kernel, lev=lev, slots=slots),
         out_shape=jax.ShapeDtypeStruct((waves * pairs, 2 * lanes), jnp.bfloat16),
         in_specs=[pl.BlockSpec(memory_space=pltpu.SMEM), any_space, any_space],
-        out_specs=any_space,
+        out_specs=pl.BlockSpec(memory_space=pltpu.VMEM),
         scratch_shapes=[
             pltpu.VMEM((pairs, lanes, columns), jnp.bfloat16),
             pltpu.VMEM((waves // 128, 128), jnp.int32),
             pltpu.VMEM((waves, waves), jnp.bfloat16),
             pltpu.VMEM((waves, 128), jnp.int32),
             pltpu.VMEM((waves * pairs, 2 * lanes), jnp.float32),
-            pltpu.VMEM((waves * pairs, 2 * lanes), jnp.bfloat16),
             pltpu.SemaphoreType.DMA((pairs // 2,)),
             pltpu.SemaphoreType.DMA,
-            pltpu.SemaphoreType.DMA((4,)),
         ],
         compiler_params=pltpu.CompilerParams(vmem_limit_bytes=60 * 1024 * 1024),
         name="pack",
@@ -229,24 +198,20 @@
         out_shape=jax.ShapeDtypeStruct((slots, sides, rows, lanes), jnp.bfloat16),
         in_specs=[
             pl.BlockSpec(memory_space=pltpu.SMEM),
-            any_space,
-            any_space,
+            pl.BlockSpec(memory_space=pltpu.VMEM),
+            pl.BlockSpec(memory_space=pltpu.VMEM),
             any_space,
         ],
         out_specs=any_space,
         scratch_shapes=[
-            pltpu.VMEM((total, lanes), jnp.bfloat16),
-            pltpu.VMEM(vertical.shape, jnp.bfloat16),
             pltpu.VMEM((slots, sides, rows, pairs), jnp.bfloat16),
             pltpu.VMEM((sides, total // lev, lanes), jnp.float32),
             [pltpu.VMEM((pairs, 2 * lanes), jnp.bfloat16)] * sides,
             pltpu.VMEM((slots, sides, rows, lanes), jnp.bfloat16),
-            pltpu.SemaphoreType.DMA((4, lev)),
-            pltpu.SemaphoreType.DMA,
             pltpu.SemaphoreType.DMA((slots,)),
             pltpu.SemaphoreType.DMA((slots,)),
         ],
-        compiler_params=pltpu.CompilerParams(vmem_limit_bytes=60 * 1024 * 1024),
+        compiler_params=pltpu.CompilerParams(vmem_limit_bytes=50 * 1024 * 1024),
         name="transform",
     )(own_waves, arrived, vertical, legendre)
 

time: 54.6 us -> 52.1 us (0.954)
  local copies, waits for them, and re-layouts: 2.92 us -> 1.04 us
  waiting for transfers between devices: 24.5 us -> 25.8 us
  Pallas kernels: 13.9 us -> 12.7 us
  other arithmetic: 0.98 us -> 0.26 us
    pallas_call x1, Pallas kernels: 9.06 us -> 7.71 us  [transform(): pl.pallas_call(functools.partial(transform_kernel, lev=lev, limit=2 * row...]
    unnamed x16 -> x14, local copies, waits for them, and re-layouts: 1.34 us -> 0.05 us
    all_to_all x1, waiting for transfers between devices: 24.5 us -> 25.8 us  [body(): lax.all_to_all(split, ('lev', 'lat'), split_axis=0, concat_axis=0, tiled=...]
    concatenate x1, other arithmetic: 0.74 us -> 0.02 us  [vertical_matrix(): return jnp.concatenate([high, value - high], axis=0).astype(jnp.bfloat16)]
    dynamic_slice x1, local copies, waits for them, and re-layouts: 1.35 us -> 0.77 us  [body(): lax.dynamic_slice_in_dim(waves, lax.axis_index(('lat', 'lev')) * slots, s...]
  transfers between devices with their start and end apart: 1 -> 1, of which waited for: 1 -> 1; matrix products, arithmetic and copies ran while one was open for 5% -> 2% of each run, Pallas kernels for 0% -> 0%
where the time goes in v3:
time: 52.1 us; the launch traced here: 51.5 us
  waiting for transfers between devices  25.8 us (50%)
  Pallas kernels  12.7 us (24%)
  starting transfers between devices  11.5 us (22%)
  local copies, waits for them, and re-layouts  1.04 us (2%)
    all_to_all x1, waiting for transfers between devices, body(): lax.all_to_all(split, ('lev', 'lat'), split_axis=0, concat_axis=0, tiled=...  25.8 us
    all_to_all x1, starting transfers between devices, body(): lax.all_to_all(split, ('lev', 'lat'), split_axis=0, concat_axis=0, tiled=...  11.5 us
    pallas_call x1, Pallas kernels, transform(): pl.pallas_call(functools.partial(transform_kernel, lev=lev, limit=2 * row...  7.71 us
    pallas_call x1, Pallas kernels, pack(): pl.pallas_call(functools.partial(pack_kernel, lev=lev, slots=slots), out_...  5 us
  transfers between devices with their start and end apart: 1, of which 1 were waited for; matrix products, arithmetic and copies ran while one was open for 2% of the time, Pallas kernels for 0%

profile of v3, /device:TPU:1, one launch (start us, length us, event | category | flops | bytes accessed | tf_op | source)
XLA Modules:
  0.0 51.5 jit_solution(9142050845233630020)
XLA Ops:
  0.0 5.0 %pack.1 = bf16[7680,128]{1,0:T(8,128)(2,1)} custom-call(s32[10]{0:T(128)} %cycles_ref.1, bf16[10,64,1536]{2,1,0:T(8,128)(2,1)} %bitcast.16, s32[6,128]{1,0:T(8,128)} %bitcast.18), custom_call_target="tpu_custom_call" | custom-call | tf_op jit(solution)/shard_map/pack/pallas_call | solution.py:173
  5.0 0.0 copy-start.6
  5.0 0.0 copy-start
  5.0 0.0 copy-start.1
  5.0 0.0 copy-start.2
  5.1 0.0 copy-start.3
  5.1 0.0 copy-start.4
  5.1 0.0 copy-start.5
  5.1 11.5 %all-to-all-start = ((bf16[128,15,4,128]{3,2,1,0:T(4,128)(2,1)}), bf16[128,15,4,128]{3,2,1,0:T(4,128)(2,1)S(1)}, u32[]{:S(2)}, u32[]{:S(2)}) async-start(bf16[128,15,4,128]{3,2,1,0:T(4,128)(2,1)} %bitcast.15), calls=%async_computation | async-start | bytes 3932160 | tf_op jit(solution)/shard_map/all_to_all | solution.py:224
  16.6 0.0 copy-done.6
  16.6 0.1 reshape.23
  16.7 0.1 reshape.24
  16.9 0.8 %dynamic_slice.3.wave_ref = s32[6]{0:T(128)S(1)} dynamic-slice(s32[768]{0:T(1024)} %param.15, s32[]{:T(128)S(6)} %select_n.19), dynamic_slice_sizes={6} | dynamic-slice | bytes 52 | tf_op jit(solution)/shard_map/dynamic_slice | solution.py:226
  17.6 0.0 copy-done
  17.6 0.0 copy-done.1
  17.6 0.0 copy-done.2
  17.7 0.0 copy-done.3
  17.7 0.0 copy-done.4
  17.7 0.0 copy-done.5
  17.7 0.2 reduce-precision_convert_fusion
  18.0 25.8 %all-to-all-done = bf16[128,15,4,128]{3,2,1,0:T(4,128)(2,1)S(1)} async-done(((bf16[128,15,4,128]{3,2,1,0:T(4,128)(2,1)}), bf16[128,15,4,128]{3,2,1,0:T(4,128)(2,1)S(1)}, u32[]{:S(2)}, u32[]{:S(2)}) %all-to-all-start) | async-done | bytes 1966112 | tf_op jit(solution)/shard_map/all_to_all | solution.py:224
  43.7 7.7 %transform.1 = bf16[6,2,640,128]{3,2,1,0:T(8,128)(2,1)} custom-call(s32[6]{0:T(128)S(1)} %dynamic_slice.3.wave_ref, bf16[7680,128]{1,0:T(8,128)(2,1)S(1)} %bitcast.14, bf16[512,256]{1,0:T(8,128)(2,1)S(1)} %pad_maximum_fusion.vertical, bf16[6,2,640,640]{3,2,1,0:T(8,128)(2,1)} %table_ref.1), custom_call_target="tpu_custom_call" | custom-call | tf_op jit(solution)/shard_map/transform/pallas_call | solution.py:196
  (4 shorter events, 0.0 us)
Async XLA Ops:
  5.0 11.6 %copy-start.6 = (f32[4,16,5]{1,0,2:T(4,128)S(1)}, f32[4,16,5]{1,0,2:T(4,128)}, u32[]{:S(2)}) copy-start(f32[4,16,5]{1,0,2:T(4,128)} %param.12) | copy-start | bytes 3844
  5.0 12.6 %copy-start = (f32[256,256]{1,0:T(8,128)S(1)}, f32[256,256]{1,0:T(8,128)}, u32[]{:S(2)}) copy-start(f32[256,256]{1,0:T(8,128)} %constant.39) | copy-start | bytes 786436
  5.0 12.6 %copy-start.1 = (pred[256,256]{1,0:T(32,128)(4,1)S(1)}, pred[256,256]{1,0:T(32,128)(4,1)}, u32[]{:S(2)}) copy-start(pred[256,256]{1,0:T(32,128)(4,1)} %constant.34.clone) | copy-start | bytes 196612
  5.0 12.6 %copy-start.2 = (pred[256,256]{1,0:T(32,128)(4,1)S(1)}, pred[256,256]{1,0:T(32,128)(4,1)}, u32[]{:S(2)}) copy-start(pred[256,256]{1,0:T(32,128)(4,1)} %constant.33.clone) | copy-start | bytes 196612
  5.1 12.6 %copy-start.3 = (pred[256,256]{1,0:T(32,128)(4,1)S(1)}, pred[256,256]{1,0:T(32,128)(4,1)}, u32[]{:S(2)}) copy-start(pred[256,256]{1,0:T(32,128)(4,1)} %constant.32.clone) | copy-start | bytes 196612
  5.1 12.6 %copy-start.4 = (pred[256,256]{1,0:T(32,128)(4,1)S(1)}, pred[256,256]{1,0:T(32,128)(4,1)}, u32[]{:S(2)}) copy-start(pred[256,256]{1,0:T(32,128)(4,1)} %constant.31.clone) | copy-start | bytes 196612
  5.1 12.6 %copy-start.5 = (pred[256,256]{1,0:T(32,128)(4,1)S(1)}, pred[256,256]{1,0:T(32,128)(4,1)}, u32[]{:S(2)}) copy-start(pred[256,256]{1,0:T(32,128)(4,1)} %constant.30.clone) | copy-start | bytes 196612
  5.1 38.6 %all-to-all-start = ((bf16[128,15,4,128]{3,2,1,0:T(4,128)(2,1)}), bf16[128,15,4,128]{3,2,1,0:T(4,128)(2,1)S(1)}, u32[]{:S(2)}, u32[]{:S(2)}) async-start(bf16[128,15,4,128]{3,2,1,0:T(4,128)(2,1)} %bitcast.15), calls=%async_computation | async-start | bytes 3932160 | tf_op jit(solution)/shard_map/all_to_all | solution.py:224

commit v4 on v3

--- a/solution.py
+++ b/solution.py
@@ -19,13 +19,10 @@
     run = pairs * slots
     group = 2
 
-    def arriving(j):
-        return pltpu.make_async_copy(fourier_ref.at[pl.ds(j, group)], fourier.at[pl.ds(j, group)], in_sem.at[j // group])
-
+    arrive = pltpu.make_async_copy(fourier_ref, fourier, in_sem)
+    arrive.start()
     arrive_wave = pltpu.make_async_copy(wave_ref, wave, wave_sem)
     arrive_wave.start()
-    for j in range(0, pairs, group):
-        arriving(j).start()
     arrive_wave.wait()
     shape = (waves // 128, 128)
     slot = lax.rem(lax.broadcasted_iota(jnp.int32, shape, 0) * 128 + lax.broadcasted_iota(jnp.int32, shape, 1), slots)
@@ -45,8 +42,8 @@
     index = lax.broadcasted_iota(jnp.int32, (1, waves), 1)
 
     def gather(columns_of):
+        arrive.wait()
         for j in range(0, pairs, group):
-            arriving(j).wait()
             blocks = []
             for i in range(j, j + group):
                 keep = 2 * index < cycles_ref[i]
@@ -83,35 +80,25 @@
 
 
 def transform_kernel(wave_ref, arrived, vertical, table_ref, out_ref,
-                     tables, folded, right, result, table_sem, out_sem, *, lev, limit):
+                     tables, folded, right, result, table_sem, out_sem, *, lev, block, limit):
     slots, sides, rows, pairs = tables.shape
     half = arrived.shape[0] // lev
-    chunks = 4
-    step = half // chunks
+    step = half // 4
     tile = 128
-    counts = range(rows // tile // 2 + 1, rows // tile + 1)
 
     def table(q, n):
         part = pl.ds(0, n * tile)
         return pltpu.make_async_copy(table_ref.at[q, :, part], tables.at[q, :, part], table_sem.at[q])
 
-    def count(q):
-        return jnp.clip((limit - wave_ref[q] + 2 * tile - 1) // (2 * tile), counts[0], counts[-1])
-
-    def start_table(q):
-        for n in counts:
-            @pl.when(count(q) == n)
-            def _():
-                table(q, n).start()
-
-    for q in range(slots):
-        start_table(q)
-    for i in range(chunks):
-        at = i * step
-        source = jnp.concatenate([arrived[pl.ds(v * half + at, step), :] for v in range(lev)] * 2, axis=1)
-        made = jnp.dot(source, vertical[...], preferred_element_type=jnp.float32)
-        for s in range(sides):
-            folded[s, pl.ds(at, step), :] = made[:, s * 128:(s + 1) * 128]
+    def leaving(q):
+        return pltpu.make_async_copy(result.at[q], out_ref.at[q], out_sem.at[q])
+
+    def fold():
+        for at in range(0, half, step):
+            source = jnp.concatenate([arrived[pl.ds(v * half + at, step), :] for v in range(lev)] * 2, axis=1)
+            made = jnp.dot(source, vertical[...], preferred_element_type=jnp.float32)
+            for s in range(sides):
+                folded[s, pl.ds(at, step), :] = made[:, s * 128:(s + 1) * 128]
 
     degree = 2 * lax.broadcasted_iota(jnp.int32, (tile, 128), 0)
 
@@ -119,29 +106,56 @@
         column = folded[s, pl.ds(q, pairs, stride=slots), :]
         right[s][...] = jnp.concatenate(split_bf16(column), axis=1)
 
-    prepare(0, 0)
-
-    @pl.loop(0, slots)
-    def _(q):
-        for n in counts:
-            @pl.when(count(q) == n)
-            def _():
-                table(q, n).wait()
-                for s in range(sides):
-                    prepare(q, 1) if s == 0 else prepare(jnp.minimum(q + 1, slots - 1), 0)
-                    for i in range(n):
-                        part = pl.ds(i * tile, tile)
-                        both = jnp.dot(tables[q, s, part], right[s][...], preferred_element_type=jnp.float32)
-                        product = both[:, :128] + both[:, 128:]
-                        valid = degree < limit - 2 * i * tile - s - wave_ref[q]
-                        result[q, s, part] = jnp.where(valid, product, 0.0).astype(jnp.bfloat16)
-                    if n * tile < rows:
-                        rest = pl.ds(n * tile, rows - n * tile)
-                        result[q, s, rest] = jnp.zeros((rows - n * tile, 128), jnp.bfloat16)
-        pltpu.make_async_copy(result.at[q], out_ref.at[q], out_sem.at[q]).start()
-
-    for q in range(slots):
-        pltpu.make_async_copy(result.at[q], out_ref.at[q], out_sem.at[q]).wait()
+    def multiply(q, s, n):
+        for i in range(n):
+            part = pl.ds(i * tile, tile)
+            both = jnp.dot(tables[q, s, part], right[s][...], preferred_element_type=jnp.float32)
+            product = both[:, :128] + both[:, 128:]
+            valid = degree < limit - 2 * i * tile - s - wave_ref[q]
+            result[q, s, part] = jnp.where(valid, product, 0.0).astype(jnp.bfloat16)
+        if n * tile < rows:
+            result[q, s, pl.ds(n * tile, rows - n * tile)] = jnp.zeros((rows - n * tile, 128), jnp.bfloat16)
+
+    counts = [min(rows // tile, -(-(limit - q * block) // (2 * tile))) for q in range(slots)]
+    fits = wave_ref[0] >= 0
+    for q in range(1, slots):
+        fits = jnp.logical_and(fits, wave_ref[q] >= q * block)
+    groups = {0: (0,), 1: (1, 2), 3: (3, 4, 5)}
+
+    @pl.when(fits)
+    def _():
+        for q in range(slots):
+            table(q, counts[q]).start()
+        fold()
+        prepare(0, 0)
+        for q in range(slots):
+            for k in groups.get(q, ()):
+                table(k, counts[k]).wait()
+            for s in range(sides):
+                after = q + (s + 1) // sides
+                if after < slots:
+                    prepare(after, (s + 1) % sides)
+                multiply(q, s, counts[q])
+            leaving(q).start()
+        for q in range(slots):
+            leaving(q).wait()
+
+    @pl.when(jnp.logical_not(fits))
+    def _():
+        for q in range(slots):
+            table(q, rows // tile).start()
+        fold()
+
+        @pl.loop(0, slots)
+        def _(q):
+            table(q, rows // tile).wait()
+            for s in range(sides):
+                prepare(q, s)
+                multiply(q, s, rows // tile)
+            leaving(q).start()
+
+        for q in range(slots):
+            leaving(q).wait()
 
 
 def vertical_matrix(band, lev):
@@ -181,7 +195,7 @@
             pltpu.VMEM((waves, waves), jnp.bfloat16),
             pltpu.VMEM((waves, 128), jnp.int32),
             pltpu.VMEM((waves * pairs, 2 * lanes), jnp.float32),
-            pltpu.SemaphoreType.DMA((pairs // 2,)),
+            pltpu.SemaphoreType.DMA,
             pltpu.SemaphoreType.DMA,
         ],
         compiler_params=pltpu.CompilerParams(vmem_limit_bytes=60 * 1024 * 1024),
@@ -189,12 +203,12 @@
     )(cycle_points, fourier.reshape(pairs, lanes, columns), wave_of_slot.reshape(waves // 128, 128))
 
 
-def transform(own_waves, arrived, vertical, legendre, lev):
+def transform(own_waves, arrived, vertical, legendre, lev, block=128):
     slots, sides, rows, pairs = legendre.shape
     total, lanes = arrived.shape
     any_space = pl.BlockSpec(memory_space=pl.ANY)
     return pl.pallas_call(
-        functools.partial(transform_kernel, lev=lev, limit=2 * rows),
+        functools.partial(transform_kernel, lev=lev, block=block, limit=2 * rows),
         out_shape=jax.ShapeDtypeStruct((slots, sides, rows, lanes), jnp.bfloat16),
         in_specs=[
             pl.BlockSpec(memory_space=pltpu.SMEM),
@@ -225,7 +239,7 @@
     vertical_band, waves = lax.optimization_barrier((vertical_band, wave_of_slot, outgoing))[:2]
     own_waves = lax.dynamic_slice_in_dim(waves, lax.axis_index(("lat", "lev")) * slots, slots)
     vertical = vertical_matrix(vertical_band, lev)
-    return transform(own_waves, arrived.reshape(outgoing.shape), vertical, legendre, lev)
+    return transform(own_waves, arrived.reshape(outgoing.shape), vertical, legendre, lev, lat * lev)
 
 
 def solution(mesh):

time: 52.1 us -> 49.8 us (0.956)
  Pallas kernels: 12.7 us -> 10.4 us
    pallas_call x1, Pallas kernels: 7.71 us -> 6.05 us  [transform(): pl.pallas_call(functools.partial(transform_kernel, lev=lev, block=block,...]
    pallas_call x1, Pallas kernels: 5 us -> 4.39 us  [pack(): pl.pallas_call(functools.partial(pack_kernel, lev=lev, slots=slots), out_...]
  transfers between devices with their start and end apart: 1 -> 1, of which waited for: 1 -> 1; matrix products, arithmetic and copies ran while one was open for 2% -> 3% of each run, Pallas kernels for 0% -> 0%
where the time goes in v4:
time: 49.8 us; the launch traced here: 49.2 us
  waiting for transfers between devices  25.8 us (52%)
  starting transfers between devices  11.5 us (23%)
  Pallas kernels  10.4 us (21%)
  local copies, waits for them, and re-layouts  1.04 us (2%)
    all_to_all x1, waiting for transfers between devices, body(): lax.all_to_all(split, ('lev', 'lat'), split_axis=0, concat_axis=0, tiled=...  25.8 us
    all_to_all x1, starting transfers between devices, body(): lax.all_to_all(split, ('lev', 'lat'), split_axis=0, concat_axis=0, tiled=...  11.5 us
    pallas_call x1, Pallas kernels, transform(): pl.pallas_call(functools.partial(transform_kernel, lev=lev, block=block,...  6.05 us
    pallas_call x1, Pallas kernels, pack(): pl.pallas_call(functools.partial(pack_kernel, lev=lev, slots=slots), out_...  4.39 us
  transfers between devices with their start and end apart: 1, of which 1 were waited for; matrix products, arithmetic and copies ran while one was open for 3% of the time, Pallas kernels for 0%

profile of v4, /device:TPU:1, one launch (start us, length us, event | category | flops | bytes accessed | tf_op | source)
XLA Modules:
  0.0 49.2 jit_solution(5183175758203539072)
XLA Ops:
  0.0 4.4 %pack.1 = bf16[7680,128]{1,0:T(8,128)(2,1)} custom-call(s32[10]{0:T(128)} %cycles_ref.1, bf16[10,64,1536]{2,1,0:T(8,128)(2,1)} %bitcast.16, s32[6,128]{1,0:T(8,128)} %bitcast.18), custom_call_target="tpu_custom_call" | custom-call | tf_op jit(solution)/shard_map/pack/pallas_call | solution.py:187
  4.4 0.0 copy-start.6
  4.4 0.0 copy-start
  4.4 0.0 copy-start.1
  4.4 0.0 copy-start.2
  4.5 0.0 copy-start.3
  4.5 0.0 copy-start.4
  4.5 0.0 copy-start.5
  4.5 11.5 %all-to-all-start = ((bf16[128,15,4,128]{3,2,1,0:T(4,128)(2,1)}), bf16[128,15,4,128]{3,2,1,0:T(4,128)(2,1)S(1)}, u32[]{:S(2)}, u32[]{:S(2)}) async-start(bf16[128,15,4,128]{3,2,1,0:T(4,128)(2,1)} %bitcast.15), calls=%async_computation | async-start | bytes 3932160 | tf_op jit(solution)/shard_map/all_to_all | solution.py:238
  16.0 0.0 copy-done.6
  16.0 0.1 reshape.23
  16.1 0.1 reshape.24
  16.3 0.8 %dynamic_slice.3.wave_ref = s32[6]{0:T(128)S(1)} dynamic-slice(s32[768]{0:T(1024)} %param.15, s32[]{:T(128)S(6)} %select_n.19), dynamic_slice_sizes={6} | dynamic-slice | bytes 52 | tf_op jit(solution)/shard_map/dynamic_slice | solution.py:240
  17.0 0.0 copy-done
  17.0 0.0 copy-done.1
  17.0 0.0 copy-done.2
  17.1 0.0 copy-done.3
  17.1 0.0 copy-done.4
  17.1 0.0 copy-done.5
  17.1 0.2 reduce-precision_convert_fusion
  17.4 25.8 %all-to-all-done = bf16[128,15,4,128]{3,2,1,0:T(4,128)(2,1)S(1)} async-done(((bf16[128,15,4,128]{3,2,1,0:T(4,128)(2,1)}), bf16[128,15,4,128]{3,2,1,0:T(4,128)(2,1)S(1)}, u32[]{:S(2)}, u32[]{:S(2)}) %all-to-all-start) | async-done | bytes 1966112 | tf_op jit(solution)/shard_map/all_to_all | solution.py:238
  43.1 6.1 %transform.1 = bf16[6,2,640,128]{3,2,1,0:T(8,128)(2,1)} custom-call(s32[6]{0:T(128)S(1)} %dynamic_slice.3.wave_ref, bf16[7680,128]{1,0:T(8,128)(2,1)S(1)} %bitcast.14, bf16[512,256]{1,0:T(8,128)(2,1)S(1)} %pad_maximum_fusion.vertical, bf16[6,2,640,640]{3,2,1,0:T(8,128)(2,1)} %table_ref.1), custom_call_target="tpu_custom_call" | custom-call | tf_op jit(solution)/shard_map/transform/pallas_call | solution.py:210
  (4 shorter events, 0.0 us)
Async XLA Ops:
  4.4 11.6 %copy-start.6 = (f32[4,16,5]{1,0,2:T(4,128)S(1)}, f32[4,16,5]{1,0,2:T(4,128)}, u32[]{:S(2)}) copy-start(f32[4,16,5]{1,0,2:T(4,128)} %param.12) | copy-start | bytes 3844
  4.4 12.6 %copy-start = (f32[256,256]{1,0:T(8,128)S(1)}, f32[256,256]{1,0:T(8,128)}, u32[]{:S(2)}) copy-start(f32[256,256]{1,0:T(8,128)} %constant.39) | copy-start | bytes 786436
  4.4 12.6 %copy-start.1 = (pred[256,256]{1,0:T(32,128)(4,1)S(1)}, pred[256,256]{1,0:T(32,128)(4,1)}, u32[]{:S(2)}) copy-start(pred[256,256]{1,0:T(32,128)(4,1)} %constant.34.clone) | copy-start | bytes 196612
  4.4 12.6 %copy-start.2 = (pred[256,256]{1,0:T(32,128)(4,1)S(1)}, pred[256,256]{1,0:T(32,128)(4,1)}, u32[]{:S(2)}) copy-start(pred[256,256]{1,0:T(32,128)(4,1)} %constant.33.clone) | copy-start | bytes 196612
  4.5 12.6 %copy-start.3 = (pred[256,256]{1,0:T(32,128)(4,1)S(1)}, pred[256,256]{1,0:T(32,128)(4,1)}, u32[]{:S(2)}) copy-start(pred[256,256]{1,0:T(32,128)(4,1)} %constant.32.clone) | copy-start | bytes 196612
  4.5 12.6 %copy-start.4 = (pred[256,256]{1,0:T(32,128)(4,1)S(1)}, pred[256,256]{1,0:T(32,128)(4,1)}, u32[]{:S(2)}) copy-start(pred[256,256]{1,0:T(32,128)(4,1)} %constant.31.clone) | copy-start | bytes 196612
  4.5 12.6 %copy-start.5 = (pred[256,256]{1,0:T(32,128)(4,1)S(1)}, pred[256,256]{1,0:T(32,128)(4,1)}, u32[]{:S(2)}) copy-start(pred[256,256]{1,0:T(32,128)(4,1)} %constant.30.clone) | copy-start | bytes 196612
  4.5 38.6 %all-to-all-start = ((bf16[128,15,4,128]{3,2,1,0:T(4,128)(2,1)}), bf16[128,15,4,128]{3,2,1,0:T(4,128)(2,1)S(1)}, u32[]{:S(2)}, u32[]{:S(2)}) async-start(bf16[128,15,4,128]{3,2,1,0:T(4,128)(2,1)} %bitcast.15), calls=%async_computation | async-start | bytes 3932160 | tf_op jit(solution)/shard_map/all_to_all | solution.py:238

commit v5 on v4

--- a/solution.py
+++ b/solution.py
@@ -12,7 +12,7 @@
 
 
 def pack_kernel(cycles_ref, fourier_ref, wave_ref, out_ref,
-                fourier, wave, pick, column_ref, rows_ref, in_sem, wave_sem, *, lev, slots):
+                fourier, wave, pick, column_ref, rows_ref, packed, in_sem, wave_sem, out_sem, *, lev, slots):
     pairs, parts, waves = fourier_ref.shape[0], 2, fourier_ref.shape[2] // 2
     holders = waves // slots
     lat = holders // lev
@@ -70,7 +70,17 @@
         fill(lambda q: range(waves // 128))
         gather(lambda q: (0, waves))
 
-    out_ref[...] = rows_ref[...].astype(jnp.bfloat16)
+    part = packed.shape[0] // out_sem.shape[0]
+
+    def leaving(i):
+        at = pl.ds(i * part, part)
+        return pltpu.make_async_copy(packed.at[at], out_ref.at[at], out_sem.at[i])
+
+    for i in range(out_sem.shape[0]):
+        packed[pl.ds(i * part, part), :] = rows_ref[pl.ds(i * part, part), :].astype(jnp.bfloat16)
+        leaving(i).start()
+    for i in range(out_sem.shape[0]):
+        leaving(i).wait()
 
 
 def split_bf16(value):
@@ -83,7 +93,7 @@
                      tables, folded, right, result, table_sem, out_sem, *, lev, block, limit):
     slots, sides, rows, pairs = tables.shape
     half = arrived.shape[0] // lev
-    step = half // 4
+    step = half // 8
     tile = 128
 
     def table(q, n):
@@ -100,18 +110,19 @@
             for s in range(sides):
                 folded[s, pl.ds(at, step), :] = made[:, s * 128:(s + 1) * 128]
 
-    degree = 2 * lax.broadcasted_iota(jnp.int32, (tile, 128), 0)
+    degree = 2 * lax.broadcasted_iota(jnp.int32, (rows, 128), 0)
 
     def prepare(q, s):
         column = folded[s, pl.ds(q, pairs, stride=slots), :]
         right[s][...] = jnp.concatenate(split_bf16(column), axis=1)
 
     def multiply(q, s, n):
-        for i in range(n):
-            part = pl.ds(i * tile, tile)
+        size = n * tile
+        for at in range(0, n * tile, size):
+            part = pl.ds(at, size)
             both = jnp.dot(tables[q, s, part], right[s][...], preferred_element_type=jnp.float32)
             product = both[:, :128] + both[:, 128:]
-            valid = degree < limit - 2 * i * tile - s - wave_ref[q]
+            valid = degree[:size] < limit - 2 * at - s - wave_ref[q]
             result[q, s, part] = jnp.where(valid, product, 0.0).astype(jnp.bfloat16)
         if n * tile < rows:
             result[q, s, pl.ds(n * tile, rows - n * tile)] = jnp.zeros((rows - n * tile, 128), jnp.bfloat16)
@@ -188,15 +199,17 @@
         functools.partial(pack_kernel, lev=lev, slots=slots),
         out_shape=jax.ShapeDtypeStruct((waves * pairs, 2 * lanes), jnp.bfloat16),
         in_specs=[pl.BlockSpec(memory_space=pltpu.SMEM), any_space, any_space],
-        out_specs=pl.BlockSpec(memory_space=pltpu.VMEM),
+        out_specs=any_space,
         scratch_shapes=[
             pltpu.VMEM((pairs, lanes, columns), jnp.bfloat16),
             pltpu.VMEM((waves // 128, 128), jnp.int32),
             pltpu.VMEM((waves, waves), jnp.bfloat16),
             pltpu.VMEM((waves, 128), jnp.int32),
             pltpu.VMEM((waves * pairs, 2 * lanes), jnp.float32),
+            pltpu.VMEM((waves * pairs, 2 * lanes), jnp.bfloat16),
             pltpu.SemaphoreType.DMA,
             pltpu.SemaphoreType.DMA,
+            pltpu.SemaphoreType.DMA((2,)),
         ],
         compiler_params=pltpu.CompilerParams(vmem_limit_bytes=60 * 1024 * 1024),
         name="pack",

time: 49.8 us -> 49.7 us (level)
  no operation moved by 1% of the time
where the time goes in v5:
time: 49.7 us; the launch traced here: 49.1 us
  waiting for transfers between devices  25.8 us (52%)
  starting transfers between devices  11.5 us (23%)
  Pallas kernels  10.3 us (21%)
  local copies, waits for them, and re-layouts  1.04 us (2%)
    all_to_all x1, waiting for transfers between devices, body(): lax.all_to_all(split, ('lev', 'lat'), split_axis=0, concat_axis=0, tiled=...  25.8 us
    all_to_all x1, starting transfers between devices, body(): lax.all_to_all(split, ('lev', 'lat'), split_axis=0, concat_axis=0, tiled=...  11.5 us
    pallas_call x1, Pallas kernels, transform(): pl.pallas_call(functools.partial(transform_kernel, lev=lev, block=block,...  6.02 us
    pallas_call x1, Pallas kernels, pack(): pl.pallas_call(functools.partial(pack_kernel, lev=lev, slots=slots), out_...  4.31 us
  transfers between devices with their start and end apart: 1, of which 1 were waited for; matrix products, arithmetic and copies ran while one was open for 3% of the time, Pallas kernels for 0%

profile of v5, /device:TPU:1, one launch (start us, length us, event | category | flops | bytes accessed | tf_op | source)
XLA Modules:
  0.0 49.1 jit_solution(14945147986844824588)
XLA Ops:
  0.0 4.3 %pack.1 = bf16[7680,128]{1,0:T(8,128)(2,1)} custom-call(s32[10]{0:T(128)} %cycles_ref.1, bf16[10,64,1536]{2,1,0:T(8,128)(2,1)} %bitcast.16, s32[6,128]{1,0:T(8,128)} %bitcast.18), custom_call_target="tpu_custom_call" | custom-call | tf_op jit(solution)/shard_map/pack/pallas_call | solution.py:198
  4.3 0.0 copy-start.6
  4.3 0.0 copy-start
  4.3 0.0 copy-start.1
  4.4 0.0 copy-start.2
  4.4 0.0 copy-start.3
  4.4 0.0 copy-start.4
  4.4 0.0 copy-start.5
  4.4 11.5 %all-to-all-start = ((bf16[128,15,4,128]{3,2,1,0:T(4,128)(2,1)}), bf16[128,15,4,128]{3,2,1,0:T(4,128)(2,1)S(1)}, u32[]{:S(2)}, u32[]{:S(2)}) async-start(bf16[128,15,4,128]{3,2,1,0:T(4,128)(2,1)} %bitcast.15), calls=%async_computation | async-start | bytes 3932160 | tf_op jit(solution)/shard_map/all_to_all | solution.py:251
  15.9 0.0 copy-done.6
  15.9 0.1 reshape.23
  16.1 0.1 reshape.24
  16.2 0.8 %dynamic_slice.3.wave_ref = s32[6]{0:T(128)S(1)} dynamic-slice(s32[768]{0:T(1024)} %param.15, s32[]{:T(128)S(6)} %select_n.19), dynamic_slice_sizes={6} | dynamic-slice | bytes 52 | tf_op jit(solution)/shard_map/dynamic_slice | solution.py:253
  16.9 0.0 copy-done
  17.0 0.0 copy-done.1
  17.0 0.0 copy-done.2
  17.0 0.0 copy-done.3
  17.0 0.0 copy-done.4
  17.0 0.0 copy-done.5
  17.0 0.2 reduce-precision_convert_fusion
  17.3 25.8 %all-to-all-done = bf16[128,15,4,128]{3,2,1,0:T(4,128)(2,1)S(1)} async-done(((bf16[128,15,4,128]{3,2,1,0:T(4,128)(2,1)}), bf16[128,15,4,128]{3,2,1,0:T(4,128)(2,1)S(1)}, u32[]{:S(2)}, u32[]{:S(2)}) %all-to-all-start) | async-done | bytes 1966112 | tf_op jit(solution)/shard_map/all_to_all | solution.py:251
  43.1 6.0 %transform.1 = bf16[6,2,640,128]{3,2,1,0:T(8,128)(2,1)} custom-call(s32[6]{0:T(128)S(1)} %dynamic_slice.3.wave_ref, bf16[7680,128]{1,0:T(8,128)(2,1)S(1)} %bitcast.14, bf16[512,256]{1,0:T(8,128)(2,1)S(1)} %pad_maximum_fusion.vertical, bf16[6,2,640,640]{3,2,1,0:T(8,128)(2,1)} %table_ref.1), custom_call_target="tpu_custom_call" | custom-call | tf_op jit(solution)/shard_map/transform/pallas_call | solution.py:223
  (4 shorter events, 0.0 us)
Async XLA Ops:
  4.3 11.6 %copy-start.6 = (f32[4,16,5]{1,0,2:T(4,128)S(1)}, f32[4,16,5]{1,0,2:T(4,128)}, u32[]{:S(2)}) copy-start(f32[4,16,5]{1,0,2:T(4,128)} %param.12) | copy-start | bytes 3844
  4.3 12.6 %copy-start = (f32[256,256]{1,0:T(8,128)S(1)}, f32[256,256]{1,0:T(8,128)}, u32[]{:S(2)}) copy-start(f32[256,256]{1,0:T(8,128)} %constant.39) | copy-start | bytes 786436
  4.3 12.6 %copy-start.1 = (pred[256,256]{1,0:T(32,128)(4,1)S(1)}, pred[256,256]{1,0:T(32,128)(4,1)}, u32[]{:S(2)}) copy-start(pred[256,256]{1,0:T(32,128)(4,1)} %constant.34.clone) | copy-start | bytes 196612
  4.4 12.6 %copy-start.2 = (pred[256,256]{1,0:T(32,128)(4,1)S(1)}, pred[256,256]{1,0:T(32,128)(4,1)}, u32[]{:S(2)}) copy-start(pred[256,256]{1,0:T(32,128)(4,1)} %constant.33.clone) | copy-start | bytes 196612
  4.4 12.6 %copy-start.3 = (pred[256,256]{1,0:T(32,128)(4,1)S(1)}, pred[256,256]{1,0:T(32,128)(4,1)}, u32[]{:S(2)}) copy-start(pred[256,256]{1,0:T(32,128)(4,1)} %constant.32.clone) | copy-start | bytes 196612
  4.4 12.6 %copy-start.4 = (pred[256,256]{1,0:T(32,128)(4,1)S(1)}, pred[256,256]{1,0:T(32,128)(4,1)}, u32[]{:S(2)}) copy-start(pred[256,256]{1,0:T(32,128)(4,1)} %constant.31.clone) | copy-start | bytes 196612
  4.4 12.6 %copy-start.5 = (pred[256,256]{1,0:T(32,128)(4,1)S(1)}, pred[256,256]{1,0:T(32,128)(4,1)}, u32[]{:S(2)}) copy-start(pred[256,256]{1,0:T(32,128)(4,1)} %constant.30.clone) | copy-start | bytes 196612
  4.4 38.6 %all-to-all-start = ((bf16[128,15,4,128]{3,2,1,0:T(4,128)(2,1)}), bf16[128,15,4,128]{3,2,1,0:T(4,128)(2,1)S(1)}, u32[]{:S(2)}, u32[]{:S(2)}) async-start(bf16[128,15,4,128]{3,2,1,0:T(4,128)(2,1)} %bitcast.15), calls=%async_computation | async-start | bytes 3932160 | tf_op jit(solution)/shard_map/all_to_all | solution.py:251

commit v6 on v5

--- a/solution.py
+++ b/solution.py
@@ -100,8 +100,8 @@
         part = pl.ds(0, n * tile)
         return pltpu.make_async_copy(table_ref.at[q, :, part], tables.at[q, :, part], table_sem.at[q])
 
-    def leaving(q):
-        return pltpu.make_async_copy(result.at[q], out_ref.at[q], out_sem.at[q])
+    def leaving(q, s):
+        return pltpu.make_async_copy(result.at[q, s], out_ref.at[q, s], out_sem.at[q, s])
 
     def fold():
         for at in range(0, half, step):
@@ -147,9 +147,10 @@
                 if after < slots:
                     prepare(after, (s + 1) % sides)
                 multiply(q, s, counts[q])
-            leaving(q).start()
-        for q in range(slots):
-            leaving(q).wait()
+                leaving(q, s).start()
+        for q in range(slots):
+            for s in range(sides):
+                leaving(q, s).wait()
 
     @pl.when(jnp.logical_not(fits))
     def _():
@@ -163,10 +164,11 @@
             for s in range(sides):
                 prepare(q, s)
                 multiply(q, s, rows // tile)
-            leaving(q).start()
-
-        for q in range(slots):
-            leaving(q).wait()
+                leaving(q, s).start()
+
+        for q in range(slots):
+            for s in range(sides):
+                leaving(q, s).wait()
 
 
 def vertical_matrix(band, lev):
@@ -236,7 +238,7 @@
             [pltpu.VMEM((pairs, 2 * lanes), jnp.bfloat16)] * sides,
             pltpu.VMEM((slots, sides, rows, lanes), jnp.bfloat16),
             pltpu.SemaphoreType.DMA((slots,)),
-            pltpu.SemaphoreType.DMA((slots,)),
+            pltpu.SemaphoreType.DMA((slots, sides)),
         ],
         compiler_params=pltpu.CompilerParams(vmem_limit_bytes=50 * 1024 * 1024),
         name="transform",

time: 49.7 us -> 49.7 us (level)
  no operation moved by 1% of the time
where the time goes in v6:
time: 49.7 us; the launch traced here: 49.1 us
  waiting for transfers between devices  25.8 us (52%)
  starting transfers between devices  11.5 us (23%)
  Pallas kernels  10.4 us (21%)
  local copies, waits for them, and re-layouts  1.04 us (2%)
    all_to_all x1, waiting for transfers between devices, body(): lax.all_to_all(split, ('lev', 'lat'), split_axis=0, concat_axis=0, tiled=...  25.8 us
    all_to_all x1, starting transfers between devices, body(): lax.all_to_all(split, ('lev', 'lat'), split_axis=0, concat_axis=0, tiled=...  11.5 us
    pallas_call x1, Pallas kernels, transform(): pl.pallas_call(functools.partial(transform_kernel, lev=lev, block=block,...  6.06 us
    pallas_call x1, Pallas kernels, pack(): pl.pallas_call(functools.partial(pack_kernel, lev=lev, slots=slots), out_...  4.31 us
  transfers between devices with their start and end apart: 1, of which 1 were waited for; matrix products, arithmetic and copies ran while one was open for 3% of the time, Pallas kernels for 0%

profile of v6, /device:TPU:1, one launch (start us, length us, event | category | flops | bytes accessed | tf_op | source)
XLA Modules:
  0.0 49.1 jit_solution(13927091593672758148)
XLA Ops:
  0.0 4.3 %pack.1 = bf16[7680,128]{1,0:T(8,128)(2,1)} custom-call(s32[10]{0:T(128)} %cycles_ref.1, bf16[10,64,1536]{2,1,0:T(8,128)(2,1)} %bitcast.16, s32[6,128]{1,0:T(8,128)} %bitcast.18), custom_call_target="tpu_custom_call" | custom-call | tf_op jit(solution)/shard_map/pack/pallas_call | solution.py:200
  4.3 0.0 copy-start.6
  4.3 0.0 copy-start
  4.3 0.0 copy-start.1
  4.4 0.0 copy-start.2
  4.4 0.0 copy-start.3
  4.4 0.0 copy-start.4
  4.4 0.0 copy-start.5
  4.4 11.5 %all-to-all-start = ((bf16[128,15,4,128]{3,2,1,0:T(4,128)(2,1)}), bf16[128,15,4,128]{3,2,1,0:T(4,128)(2,1)S(1)}, u32[]{:S(2)}, u32[]{:S(2)}) async-start(bf16[128,15,4,128]{3,2,1,0:T(4,128)(2,1)} %bitcast.15), calls=%async_computation | async-start | bytes 3932160 | tf_op jit(solution)/shard_map/all_to_all | solution.py:253
  15.9 0.0 copy-done.6
  15.9 0.1 reshape.23
  16.1 0.1 reshape.24
  16.2 0.8 %dynamic_slice.3.wave_ref = s32[6]{0:T(128)S(1)} dynamic-slice(s32[768]{0:T(1024)} %param.15, s32[]{:T(128)S(6)} %select_n.19), dynamic_slice_sizes={6} | dynamic-slice | bytes 52 | tf_op jit(solution)/shard_map/dynamic_slice | solution.py:255
  16.9 0.0 copy-done
  17.0 0.0 copy-done.1
  17.0 0.0 copy-done.2
  17.0 0.0 copy-done.3
  17.0 0.0 copy-done.4
  17.0 0.0 copy-done.5
  17.0 0.2 reduce-precision_convert_fusion
  17.3 25.8 %all-to-all-done = bf16[128,15,4,128]{3,2,1,0:T(4,128)(2,1)S(1)} async-done(((bf16[128,15,4,128]{3,2,1,0:T(4,128)(2,1)}), bf16[128,15,4,128]{3,2,1,0:T(4,128)(2,1)S(1)}, u32[]{:S(2)}, u32[]{:S(2)}) %all-to-all-start) | async-done | bytes 1966112 | tf_op jit(solution)/shard_map/all_to_all | solution.py:253
  43.1 6.1 %transform.1 = bf16[6,2,640,128]{3,2,1,0:T(8,128)(2,1)} custom-call(s32[6]{0:T(128)S(1)} %dynamic_slice.3.wave_ref, bf16[7680,128]{1,0:T(8,128)(2,1)S(1)} %bitcast.14, bf16[512,256]{1,0:T(8,128)(2,1)S(1)} %pad_maximum_fusion.vertical, bf16[6,2,640,640]{3,2,1,0:T(8,128)(2,1)} %table_ref.1), custom_call_target="tpu_custom_call" | custom-call | tf_op jit(solution)/shard_map/transform/pallas_call | solution.py:225
  (4 shorter events, 0.0 us)
Async XLA Ops:
  4.3 11.6 %copy-start.6 = (f32[4,16,5]{1,0,2:T(4,128)S(1)}, f32[4,16,5]{1,0,2:T(4,128)}, u32[]{:S(2)}) copy-start(f32[4,16,5]{1,0,2:T(4,128)} %param.12) | copy-start | bytes 3844
  4.3 12.6 %copy-start = (f32[256,256]{1,0:T(8,128)S(1)}, f32[256,256]{1,0:T(8,128)}, u32[]{:S(2)}) copy-start(f32[256,256]{1,0:T(8,128)} %constant.39) | copy-start | bytes 786436
  4.3 12.6 %copy-start.1 = (pred[256,256]{1,0:T(32,128)(4,1)S(1)}, pred[256,256]{1,0:T(32,128)(4,1)}, u32[]{:S(2)}) copy-start(pred[256,256]{1,0:T(32,128)(4,1)} %constant.34.clone) | copy-start | bytes 196612
  4.4 12.6 %copy-start.2 = (pred[256,256]{1,0:T(32,128)(4,1)S(1)}, pred[256,256]{1,0:T(32,128)(4,1)}, u32[]{:S(2)}) copy-start(pred[256,256]{1,0:T(32,128)(4,1)} %constant.33.clone) | copy-start | bytes 196612
  4.4 12.6 %copy-start.3 = (pred[256,256]{1,0:T(32,128)(4,1)S(1)}, pred[256,256]{1,0:T(32,128)(4,1)}, u32[]{:S(2)}) copy-start(pred[256,256]{1,0:T(32,128)(4,1)} %constant.32.clone) | copy-start | bytes 196612
  4.4 12.6 %copy-start.4 = (pred[256,256]{1,0:T(32,128)(4,1)S(1)}, pred[256,256]{1,0:T(32,128)(4,1)}, u32[]{:S(2)}) copy-start(pred[256,256]{1,0:T(32,128)(4,1)} %constant.31.clone) | copy-start | bytes 196612
  4.4 12.6 %copy-start.5 = (pred[256,256]{1,0:T(32,128)(4,1)S(1)}, pred[256,256]{1,0:T(32,128)(4,1)}, u32[]{:S(2)}) copy-start(pred[256,256]{1,0:T(32,128)(4,1)} %constant.30.clone) | copy-start | bytes 196612
  4.4 38.6 %all-to-all-start = ((bf16[128,15,4,128]{3,2,1,0:T(4,128)(2,1)}), bf16[128,15,4,128]{3,2,1,0:T(4,128)(2,1)S(1)}, u32[]{:S(2)}, u32[]{:S(2)}) async-start(bf16[128,15,4,128]{3,2,1,0:T(4,128)(2,1)} %bitcast.15), calls=%async_computation | async-start | bytes 3932160 | tf_op jit(solution)/shard_map/all_to_all | solution.py:253
